TPU v7x, 128 devices: a whole 4x4x4 slice. The times are simulated.
128 devices in a mesh: rep: 4 (over y), fsdp: 32 (over x, z, core).
Axes of the slice: x: 4, y: 4, z: 4, core: 2. Of those that a mesh axis runs over, the one named last changes fastest.
Arguments:
- grads: bfloat16 [4, 12, 1024, 5120], P('rep', None, 'fsdp'), may hold values from -0.75 to 0.75
- stat_left: float32 [128, 1024, 1024], P(('rep', 'fsdp')), may hold values from -4 to 80
- stat_right: float32 [128, 1024, 1024], P(('rep', 'fsdp')), may hold values from -4 to 80
- root_left: bfloat16 [128, 1024, 1024], P(('rep', 'fsdp')), may hold values from -0.125 to 1.203125
- root_right: bfloat16 [128, 1024, 1024], P(('rep', 'fsdp')), may hold values from -0.125 to 1.203125
- owner_block: int32 [128], replicated, may hold values from -1 to 59, as said below
Outputs:
- stat_left_new: float32 [128, 1024, 1024], P(('rep', 'fsdp'))
- stat_right_new: float32 [128, 1024, 1024], P(('rep', 'fsdp'))
- update: bfloat16 [12, 1024, 5120], P(None, ('rep', 'fsdp'))
Inputs may be any that keep to these rules, and one draw needn't show every extreme that they name: `owner_block`: entry d is the block whose preconditioner owner d holds, or -1 where it holds none; each block 0 to 59 appears exactly once.
All inputs are finite; a program needn't handle non-finite values.
Results may differ from a plain program's by a relative error of at most 0.017.
Values may be sent and summed in bfloat16 or wider, within the bound.
No kernel may reach another device: no remote copies, remote signals or barrier semaphores. Data moves between devices by JAX's collectives and lax.ppermute only.
A program may use at most 128 MiB of HBM per device.

v0:
```python
import jax
import jax.numpy as jnp
from jax import lax
from jax.sharding import PartitionSpec as P

DECAY = 0.95
EPSILON = 1e-06


def to_blocks(row_pieces, columns, block_size):
    groups, height, full_width = row_pieces.shape
    shaped = row_pieces.reshape(groups, height, columns, block_size).transpose(0, 2, 1, 3)
    return shaped.reshape(groups * columns, height, block_size)


def precondition(grad_block, left_old, right_old, left_root, right_root):
    gram_left = lax.dot_general(
        grad_block, grad_block, (((1,), (1,)), ((), ())), preferred_element_type=jnp.float32
    )
    gram_right = lax.dot_general(
        grad_block, grad_block, (((0,), (0,)), ((), ())), preferred_element_type=jnp.float32
    )
    middle = jnp.dot(left_root, grad_block, preferred_element_type=jnp.float32).astype(jnp.bfloat16)
    precond = jnp.dot(middle, right_root, preferred_element_type=jnp.float32)
    as_float = grad_block.astype(jnp.float32)
    graft_scale = jnp.sqrt(jnp.mean(as_float * as_float) / (jnp.mean(precond * precond) + EPSILON))
    new_left = DECAY * left_old + (1.0 - DECAY) * gram_left
    new_right = DECAY * right_old + (1.0 - DECAY) * gram_right
    return (new_left, new_right, (precond * graft_scale).astype(jnp.bfloat16))


def body(grads, stat_left, stat_right, root_left, root_right, owner_block):
    fsdp_count = lax.axis_size("fsdp")
    rep_count = lax.axis_size("rep")
    devices = fsdp_count * rep_count
    block_size = stat_left.shape[1]
    groups = grads.shape[1]
    full_width = grads.shape[3]
    columns = full_width // block_size
    row_share = block_size // devices
    occupied = owner_block >= 0
    block_ids = jnp.maximum(owner_block, 0)
    reduced = lax.psum_scatter(
        grads[0].astype(jnp.float32).astype(jnp.bfloat16), "rep", scatter_dimension=1, tiled=True
    )
    chosen = jnp.take(to_blocks(reduced, columns, block_size), block_ids, axis=0)
    sending = jnp.where(occupied[:, None, None], chosen, jnp.zeros_like(chosen))
    piece_rows = sending.shape[1]
    arrived = lax.all_to_all(sending, ("rep", "fsdp"), split_axis=0, concat_axis=0, tiled=True)
    arrived = arrived.reshape(rep_count, fsdp_count, piece_rows, block_size)
    rep_axis = 0
    grad_block = jnp.moveaxis(arrived, rep_axis, 1).reshape(block_size, block_size)
    new_left, new_right, update_block = precondition(
        grad_block, stat_left[0], stat_right[0], root_left[0], root_right[0]
    )
    returned = lax.all_to_all(
        update_block.reshape(devices, row_share, block_size),
        ("rep", "fsdp"),
        split_axis=0,
        concat_axis=0,
        tiled=True,
    )
    blocks_total = groups * columns
    matches = owner_block[None, :] == lax.iota(jnp.int32, blocks_total)[:, None]
    owners = jnp.sum(jnp.where(matches, lax.iota(jnp.int32, devices)[None, :], 0), axis=1)
    returned_pieces = jnp.take(returned, owners, axis=0)
    update = (
        returned_pieces.reshape(groups, columns, row_share, block_size)
        .transpose(0, 2, 1, 3)
        .reshape(groups, row_share, full_width)
    )
    return (new_left[None], new_right[None], update)


def solution(mesh):
    in_specs = (
        P("rep", None, "fsdp", None),
        P(("rep", "fsdp"), None, None),
        P(("rep", "fsdp"), None, None),
        P(("rep", "fsdp"), None, None),
        P(("rep", "fsdp"), None, None),
        P(),
    )
    out_specs = (
        P(("rep", "fsdp"), None, None),
        P(("rep", "fsdp"), None, None),
        P(None, ("rep", "fsdp"), None),
    )
    return jax.shard_map(body, mesh=mesh, in_specs=in_specs, out_specs=out_specs, check_vma=False)
```

profile of v0, /device:TPU:1, one launch (start us, length us, event | category | flops | bytes accessed | tf_op | source)
XLA Modules:
  0.0 173.1 jit_solution(2832184483995761896)
XLA Ops:
  7.2 0.0 copy-start
  7.2 0.0 reduce-scatter.4.cloned.1.call-start
  7.2 4.5 %copy.21 = bf16[4,8,12,5120]{3,1,2,0:T(8,128)(2,1)} copy(bf16[4,8,12,5120]{3,1,0,2:T(8,128)(2,1)} %bitcast.64) | data formatting | bytes 7864320
  11.7 0.0 copy-start.3
  11.7 0.0 reduce-scatter.4.cloned.1.call-update
  11.7 0.6 copy-done.3
  12.4 47.4 %reduce-scatter.4.cloned.1.call-done = bf16[8,61440]{1,0:T(8,128)(2,1)} async-done(((bf16[32,61440]{1,0:T(8,128)(2,1)}), bf16[8,61440]{1,0:T(8,128)(2,1)}) %reduce-scatter.4.cloned.1.call-update) | async-done | bytes 983056
  59.8 2.0 %reshape.79 = bf16[8,12,5120]{2,1,0:T(8,128)(2,1)S(1)} reshape(bf16[8,61440]{1,0:T(8,128)(2,1)} %reduce-scatter.4.cloned.1.call-done) | data formatting | bytes 1966080
  61.8 0.1 fusion.16
  62.0 0.1 copy_dynamic-update-slice_fusion.4
  62.1 0.1 copy_dynamic-update-slice_fusion.3
  62.2 0.1 copy_dynamic-update-slice_fusion.2
  62.3 0.1 copy_dynamic-update-slice_fusion.1
  62.5 0.1 copy_dynamic-update-slice_fusion
  62.6 2.0 %gather_fusion = bf16[128,8,1024]{2,1,0:T(8,128)(2,1)} fusion(bf16[60,8,1024]{2,1,0:T(8,128)(2,1)S(1)} %bitcast.61, s32[1024]{0:T(1024)S(1)} %pad_clamp_fusion.1), kind=kCustom, calls=%fused_computation | custom fusion | bytes 4194816 | tf_op jit(solution)/shard_map/jit(_take)/gather | solution.py:46
  64.6 3.0 %select_select_fusion = bf16[128,8,1024]{2,1,0:T(8,128)(2,1)} fusion(bf16[128,8,1024]{2,1,0:T(8,128)(2,1)} %gather_fusion, pred[128]{0:T(512)(128)(4,1)S(1)} %get-tuple-element.9, pred[128]{0:T(512)(128)(4,1)S(1)} %get-tuple-element.8), kind=kLoop, calls=%fused_computation.17 | loop fusion | flops 2097152 | bytes 4194560 | tf_op jit(solution)/shard_map/jit(_where)/select_n | solution.py:47
  67.5 8.4 %all-to-all-start = ((bf16[128,8,1024]{2,1,0:T(8,128)(2,1)}), bf16[128,8,1024]{2,1,0:T(8,128)(2,1)}, u32[]{:S(2)}, u32[]{:S(2)}) async-start(bf16[128,8,1024]{2,1,0:T(8,128)(2,1)} %select_select_fusion), calls=%async_computation | async-start | bytes 4194304 | tf_op jit(solution)/shard_map/all_to_all | solution.py:49
  76.0 0.1 select_reduce_fusion
  76.1 0.1 reduce_sum.32
  76.2 29.7 %all-to-all-done = bf16[128,8,1024]{2,1,0:T(8,128)(2,1)} async-done(((bf16[128,8,1024]{2,1,0:T(8,128)(2,1)}), bf16[128,8,1024]{2,1,0:T(8,128)(2,1)}, u32[]{:S(2)}, u32[]{:S(2)}) %all-to-all-start) | async-done | bytes 2097184 | tf_op jit(solution)/shard_map/all_to_all | solution.py:49
  105.8 3.2 %copy.12 = bf16[4,32,8,1024]{3,2,0,1:T(8,128)(2,1)} copy(bf16[4,32,8,1024]{3,2,1,0:T(8,128)(2,1)} %bitcast.3) | data formatting | bytes 4194304 | tf_op jit(solution)/shard_map/reshape | solution.py:50
  109.0 3.2 %multiply_reduce_fusion.1 = f32[]{:T(128)} fusion(bf16[4,32,8,1024]{3,2,1,0:T(8,128)(2,1)} %bitcast.3), kind=kLoop, calls=%fused_computation.9 | loop fusion | flops 3145727 | bytes 2097156 | tf_op jit(solution)/shard_map/reduce_sum | solution.py:26
  112.2 0.0 copy-done
  112.2 9.5 %multiply_reduce_fusion = (f32[]{:T(128)}, f32[1024,1024]{1,0:T(8,128)}) fusion(bf16[1,1024,1024]{2,1,0:T(8,128)(2,1)S(1)} %copy-done, bf16[1024,1024]{1,0:T(8,128)(2,1)} %bitcast.65, bf16[1,1024,1024]{2,1,0:T(8,128)(2,1)} %param.9), kind=kOutput, calls=%fused_computation.8 | convolution fusion | flops 4298113024 | bytes 10485764 | tf_op jit(solution)/shard_map/dot_general | solution.py:24
  123.0 4.1 %fusion.3 = bf16[128,8,1024]{2,1,0:T(8,128)(2,1)} fusion(f32[1024,1024]{1,0:T(8,128)} %get-tuple-element.11, f32[]{:T(128)S(6)} %sqrt.3), kind=kLoop, calls=%fused_computation.10 | loop fusion | flops 2097152 | bytes 6291460 | tf_op jit(solution)/shard_map/reshape | solution.py:57
  127.1 5.8 %all-to-all-start.1 = ((bf16[128,8,1024]{2,1,0:T(8,128)(2,1)}), bf16[128,8,1024]{2,1,0:T(8,128)(2,1)}, u32[]{:S(2)}, u32[]{:S(2)}) async-start(bf16[128,8,1024]{2,1,0:T(8,128)(2,1)} %fusion.3), calls=%async_computation.1 | async-start | bytes 4194304 | tf_op jit(solution)/shard_map/all_to_all | solution.py:56
  132.9 0.0 copy-start.1
  132.9 0.0 copy-start.2
  132.9 8.2 %fusion.1 = f32[1,1024,1024]{2,1,0:T(8,128)} fusion(f32[1,1024,1024]{2,1,0:T(8,128)} %param.8, bf16[4,32,8,1024]{3,2,1,0:T(8,128)(2,1)} %bitcast.3), kind=kOutput, calls=%fused_computation.4 | convolution fusion | flops 2150629376 | bytes 10485760 | tf_op jit(solution)/shard_map/dot_general | solution.py:20
  141.2 0.0 copy-done.1
  141.2 0.0 copy-done.2
  141.2 4.5 %fusion.2 = f32[1,1024,1024]{2,1,0:T(8,128)} fusion(f32[1,1024,1024]{2,1,0:T(8,128)S(1)} %copy-done.2, bf16[1024,1024]{1,0:T(8,128)(2,1)S(1)} %bitcast.66), kind=kOutput, calls=%fused_computation.6 | convolution fusion | flops 2150629376 | bytes 10485760 | tf_op jit(solution)/shard_map/dot_general | solution.py:17
  145.7 17.2 %all-to-all-done.1 = bf16[128,8,1024]{2,1,0:T(8,128)(2,1)} async-done(((bf16[128,8,1024]{2,1,0:T(8,128)(2,1)}), bf16[128,8,1024]{2,1,0:T(8,128)(2,1)}, u32[]{:S(2)}, u32[]{:S(2)}) %all-to-all-start.1) | async-done | bytes 2097184 | tf_op jit(solution)/shard_map/all_to_all | solution.py:56
  162.9 2.2 %gather_fusion.1 = bf16[60,8,1024]{2,1,0:T(8,128)(2,1)S(1)} fusion(bf16[128,8,1024]{2,1,0:T(8,128)(2,1)} %all-to-all-done.1, s32[1024]{0:T(1024)S(1)} %pad_clamp_fusion), kind=kCustom, calls=%fused_computation.1 | custom fusion | bytes 1966320 | tf_op jit(solution)/shard_map/jit(_take)/gather | solution.py:66
  165.2 1.1 broadcast_select_fusion
  (6 shorter events, 0.0 us)
Async XLA Ops:
  7.2 105.1 %copy-start = (bf16[1,1024,1024]{2,1,0:T(8,128)(2,1)S(1)}, bf16[1,1024,1024]{2,1,0:T(8,128)(2,1)}, u32[]{:S(2)}) copy-start(bf16[1,1024,1024]{2,1,0:T(8,128)(2,1)} %param.10) | copy-start | bytes 6291460
  7.2 52.7 %reduce-scatter.4.cloned.1.call-start = ((), (), s32[]{:S(2)}) async-start(), calls=%async_computation.3 | async-start | bytes 4915200
  11.7 0.7 copy-start.3
  67.5 38.3 %all-to-all-start = ((bf16[128,8,1024]{2,1,0:T(8,128)(2,1)}), bf16[128,8,1024]{2,1,0:T(8,128)(2,1)}, u32[]{:S(2)}, u32[]{:S(2)}) async-start(bf16[128,8,1024]{2,1,0:T(8,128)(2,1)} %select_select_fusion), calls=%async_computation | async-start | bytes 4194304 | tf_op jit(solution)/shard_map/all_to_all | solution.py:49
  127.1 35.8 %all-to-all-start.1 = ((bf16[128,8,1024]{2,1,0:T(8,128)(2,1)}), bf16[128,8,1024]{2,1,0:T(8,128)(2,1)}, u32[]{:S(2)}, u32[]{:S(2)}) async-start(bf16[128,8,1024]{2,1,0:T(8,128)(2,1)} %fusion.3), calls=%async_computation.1 | async-start | bytes 4194304 | tf_op jit(solution)/shard_map/all_to_all | solution.py:56
  132.9 8.2 %copy-start.1 = (bf16[4,32,8,1024]{3,2,0,1:T(8,128)(2,1)S(1)}, bf16[4,32,8,1024]{3,2,0,1:T(8,128)(2,1)}, u32[]{:S(2)}) copy-start(bf16[4,32,8,1024]{3,2,0,1:T(8,128)(2,1)} %copy.12) | copy-start | bytes 6291460
  132.9 8.2 %copy-start.2 = (f32[1,1024,1024]{2,1,0:T(8,128)S(1)}, f32[1,1024,1024]{2,1,0:T(8,128)}, u32[]{:S(2)}) copy-start(f32[1,1024,1024]{2,1,0:T(8,128)} %param.7) | copy-start | bytes 12582916
Sparse Core Ops, SparseCore 0:
  11.9 47.9 reduce-scatter.3
where the time goes:
time: 174 us; the launch traced here: 173 us
  waiting for transfers between devices  94.4 us (54%)
  matrix products  22.3 us (13%)
  between operations  15.4 us (9%)
  local copies, waits for them, and re-layouts  15.3 us (9%)
  starting transfers between devices  14.2 us (8%)
  other arithmetic  11.5 us (7%)
    unnamed x2, waiting for transfers between devices  47.5 us
    all_to_all x1, waiting for transfers between devices, body(): lax.all_to_all(sending, ('rep', 'fsdp'), split_axis=0, concat_axis=0, til...  29.7 us
    all_to_all x1, waiting for transfers between devices, body(): lax.all_to_all(update_block.reshape(devices, row_share, block_size), ('re...  17.2 us
    dot_general x1, matrix products, precondition(): precond = jnp.dot(middle, right_root, preferred_element_type=jnp.float32)  9.52 us
    all_to_all x1, starting transfers between devices, body(): lax.all_to_all(sending, ('rep', 'fsdp'), split_axis=0, concat_axis=0, til...  8.41 us
    dot_general x1, matrix products, precondition(): lax.dot_general(grad_block, grad_block, (((0,), (0,)), ((), ())), preferr...  8.21 us
    unnamed x14, local copies, waits for them, and re-layouts  7.6 us
    all_to_all x1, starting transfers between devices, body(): lax.all_to_all(update_block.reshape(devices, row_share, block_size), ('re...  5.78 us
  transfers between devices with their start and end apart: 3, of which 3 were waited for; matrix products, arithmetic and copies ran while one was open for 7% of the time, Pallas kernels for 0%

commit v1 on v0

v1 whole, which is shorter than its diff:
```python
import functools

import jax
import jax.numpy as jnp
from jax import lax
from jax.experimental import pallas as pl
from jax.experimental.pallas import tpu as pltpu
from jax.sharding import PartitionSpec as P

DECAY = 0.95
EPSILON = 1e-06
MIB = 1 << 20


def params(mib):
    return pltpu.CompilerParams(vmem_limit_bytes=mib * MIB)


def pack_kernel(strips, grads, out, sem, *, half, groups, columns, reps, width):
    copies = []
    for which in range(2):
        for column in range(columns):
            offset = pl.multiple_of((column * reps + strips[which]) * width, width)
            copies.append(
                pltpu.make_async_copy(
                    grads.at[0, pl.ds(half * groups, groups), :, pl.ds(offset, width)],
                    out.at[which, column],
                    sem.at[which * columns + column],
                )
            )
    for copy in copies:
        copy.start()
    for copy in copies:
        copy.wait()


def pack(grads, strips, half, columns, width):
    reps, groups = 4, grads.shape[1] // 2
    return pl.pallas_call(
        functools.partial(pack_kernel, half=half, groups=groups, columns=columns, reps=reps, width=width),
        out_shape=jax.ShapeDtypeStruct((2, columns, groups, grads.shape[2], width), grads.dtype),
        in_specs=[pl.BlockSpec(memory_space=pltpu.SMEM), pl.BlockSpec(memory_space=pl.ANY)],
        out_specs=pl.BlockSpec(memory_space=pl.ANY),
        scratch_shapes=[pltpu.SemaphoreType.DMA((2 * columns,))],
        compiler_params=params(16),
        name="pack",
    )(strips, grads)


def first_sum_kernel(strips, own, passing, received, kept, sending):
    del strips
    kept[0] = (own[0].astype(jnp.float32) + received[0, 0].astype(jnp.float32)).astype(kept.dtype)
    sending[0] = (passing[0].astype(jnp.float32) + received[1, 0].astype(jnp.float32)).astype(sending.dtype)


def first_sum(grads, received, strips, half):
    _, columns, groups, height, width = received.shape
    reps = 4
    piece = (1, groups, height, width)
    result = jax.ShapeDtypeStruct((columns, groups, height, width), received.dtype)
    return pl.pallas_call(
        first_sum_kernel,
        grid_spec=pltpu.PrefetchScalarGridSpec(
            num_scalar_prefetch=1,
            grid=(columns,),
            in_specs=[
                pl.BlockSpec(piece, lambda c, s: (0, half, 0, c * reps + s[0])),
                pl.BlockSpec(piece, lambda c, s: (0, half, 0, c * reps + s[1])),
                pl.BlockSpec((2,) + piece, lambda c, s: (0, c, 0, 0, 0)),
            ],
            out_specs=[pl.BlockSpec(piece, lambda c, s: (c, 0, 0, 0))] * 2,
        ),
        out_shape=[result, result],
        compiler_params=params(16),
        name="first_sum",
    )(strips, grads, grads, received)


def second_sum_kernel(owners, kept_0, received_0, kept_1, received_1, out, *, columns, groups):
    out[...] = jnp.zeros_like(out)
    for half, (kept, received) in enumerate(((kept_0, received_0), (kept_1, received_1))):
        for group in range(groups):
            for column in range(columns):
                owner = owners[(half * groups + group) * columns + column]
                total = kept[column, group].astype(jnp.float32) + received[column, group].astype(jnp.float32)
                out[owner] = total.astype(out.dtype)


def second_sum(owners, kept, received, devices):
    columns, groups, height, width = kept[0].shape
    return pl.pallas_call(
        functools.partial(second_sum_kernel, columns=columns, groups=groups),
        out_shape=jax.ShapeDtypeStruct((devices, height, width), kept[0].dtype),
        in_specs=[pl.BlockSpec(memory_space=pltpu.SMEM)] + [pl.BlockSpec(memory_space=pltpu.VMEM)] * 4,
        out_specs=pl.BlockSpec(memory_space=pltpu.VMEM),
        compiler_params=params(16),
        name="second_sum",
    )(owners, kept[0], received[0], kept[1], received[1])


def update_kernel(left, grad, right, out, precond, square, *, tiles):
    step = pl.program_id(0)
    strips, size, _ = grad.shape
    rows = size // tiles

    @pl.when(step == 0)
    def _():
        square[...] = jnp.zeros_like(square)

    middle = jnp.concatenate(
        [
            jnp.dot(left[0], grad[strip], preferred_element_type=jnp.float32).astype(jnp.bfloat16)
            for strip in range(strips)
        ],
        axis=1,
    )
    part = jnp.dot(middle, right[0], preferred_element_type=jnp.float32)
    precond[pl.ds(pl.multiple_of(step * rows, rows), rows), :] = part
    square[...] += jnp.sum((part * part).reshape(rows // 8, 8, size), axis=0)

    @pl.when(step == tiles - 1)
    def _():
        grad_square = jnp.zeros((8, grad.shape[2]), jnp.float32)
        for strip in range(strips):
            as_float = grad[strip].astype(jnp.float32)
            grad_square += jnp.sum((as_float * as_float).reshape(size // 8, 8, -1), axis=0)
        entries = size * size
        mean_grad = jnp.sum(grad_square) / entries
        mean_precond = jnp.sum(square[...]) / entries
        scale = jnp.sqrt(jnp.full((8, 128), mean_grad) / (jnp.full((8, 128), mean_precond) + EPSILON))
        out[...] = (precond[...] * scale[0:1, 0:1]).astype(out.dtype)


def block_update(left, grad, right, tiles=2):
    strips, size, width = grad.shape
    rows = size // tiles
    return pl.pallas_call(
        functools.partial(update_kernel, tiles=tiles),
        grid=(tiles,),
        out_shape=jax.ShapeDtypeStruct((size, size), jnp.bfloat16),
        in_specs=[
            pl.BlockSpec((1, rows, size), lambda t: (0, t, 0)),
            pl.BlockSpec((strips, size, width), lambda t: (0, 0, 0)),
            pl.BlockSpec((1, size, size), lambda t: (0, 0, 0)),
        ],
        out_specs=pl.BlockSpec((size, size), lambda t: (0, 0)),
        scratch_shapes=[pltpu.VMEM((size, size), jnp.float32), pltpu.VMEM((8, size), jnp.float32)],
        compiler_params=params(32),
        cost_estimate=pl.CostEstimate(flops=4 * size**3, bytes_accessed=8 * size * size, transcendentals=0),
        name="block_update",
    )(left, grad, right)


def statistics_kernel(grad, left, right, new_left, new_right):
    step = pl.program_id(0)
    strips, size, width = grad.shape
    rows = pl.ds(pl.multiple_of(step * width, width), width)
    gram = jnp.zeros((width, size), jnp.float32)
    for strip in range(strips):
        gram += lax.dot_general(
            grad[strip, rows, :], grad[strip], (((1,), (1,)), ((), ())), preferred_element_type=jnp.float32
        )
    new_left[0] = DECAY * left[0] + (1.0 - DECAY) * gram
    for strip in range(strips):
        columns = slice(strip * width, (strip + 1) * width)
        gram = lax.dot_general(
            grad[step], grad[strip], (((0,), (0,)), ((), ())), preferred_element_type=jnp.float32
        )
        new_right[0, :, columns] = DECAY * right[0, :, columns] + (1.0 - DECAY) * gram


def statistics(grad, left, right):
    strips, size, width = grad.shape
    rows = pl.BlockSpec((1, width, size), lambda t: (0, t, 0))
    return pl.pallas_call(
        statistics_kernel,
        grid=(strips,),
        out_shape=[jax.ShapeDtypeStruct(left.shape, left.dtype)] * 2,
        in_specs=[pl.BlockSpec((strips, size, width), lambda t: (0, 0, 0)), rows, rows],
        out_specs=[rows, rows],
        compiler_params=params(32),
        cost_estimate=pl.CostEstimate(flops=4 * size**3, bytes_accessed=18 * size * size, transcendentals=0),
        name="statistics",
    )(grad, left, right)


def pick_kernel(owners, returned, out, sem, *, columns, size):
    groups = out.shape[0]
    copies = []
    for group in range(groups):
        for column in range(columns):
            block = group * columns + column
            copies.append(
                pltpu.make_async_copy(
                    returned.at[owners[block]],
                    out.at[group, :, pl.ds(column * size, size)],
                    sem.at[block],
                )
            )
    for copy in copies:
        copy.start()
    for copy in copies:
        copy.wait()


def pick(owners, returned, groups, columns):
    _, rows, size = returned.shape
    return pl.pallas_call(
        functools.partial(pick_kernel, columns=columns, size=size),
        out_shape=jax.ShapeDtypeStruct((groups, rows, columns * size), returned.dtype),
        in_specs=[pl.BlockSpec(memory_space=pltpu.SMEM), pl.BlockSpec(memory_space=pl.ANY)],
        out_specs=pl.BlockSpec(memory_space=pl.ANY),
        scratch_shapes=[pltpu.SemaphoreType.DMA((groups * columns,))],
        compiler_params=params(16),
        name="pick",
    )(owners, returned)


def body(grads, stat_left, stat_right, root_left, root_right, owner_block):
    reps = lax.axis_size("rep")
    devices = lax.axis_size("fsdp") * reps
    size = stat_left.shape[1]
    groups, full_width = grads.shape[1], grads.shape[3]
    columns = full_width // size
    width = size // reps
    me = lax.axis_index("rep")
    across = [(r, r ^ 1) for r in range(reps)]
    mirror = [(r, reps - 1 - r) for r in range(reps)]
    orders = ((across, mirror), (mirror, across))
    firsts = (me ^ 1, reps - 1 - me)

    matches = owner_block[None, :] == lax.iota(jnp.int32, groups * columns)[:, None]
    owners = jnp.sum(jnp.where(matches, lax.iota(jnp.int32, devices)[None, :], 0), axis=1)

    kept, received = [], []
    arrived = []
    for half in range(2):
        partner = firsts[half]
        partner_second = (reps - 1 - partner, partner ^ 1)[half]
        packed = pack(grads, jnp.stack([partner, partner_second]).astype(jnp.int32), half, columns, width)
        arrived.append(lax.ppermute(packed, "rep", orders[half][0]))
    for half in range(2):
        own_second = (reps - 1 - me, me ^ 1)[half]
        keep, sending = first_sum(grads, arrived[half], jnp.stack([me, own_second]).astype(jnp.int32), half)
        kept.append(keep)
        received.append(lax.ppermute(sending, "rep", orders[half][1]))
    pieces = second_sum(owners, kept, received, devices)
    grad_block = lax.all_to_all(pieces, ("rep", "fsdp"), split_axis=0, concat_axis=0, tiled=True)
    grad_block = grad_block.reshape(reps, size, width)
    update_block = block_update(root_left, grad_block, root_right)
    returned = lax.all_to_all(
        update_block.reshape(devices, size // devices, size),
        ("rep", "fsdp"),
        split_axis=0,
        concat_axis=0,
        tiled=True,
    )
    new_left, new_right = statistics(grad_block, stat_left, stat_right)
    return (new_left, new_right, pick(owners, returned, groups, columns))


def solution(mesh):
    in_specs = (
        P("rep", None, "fsdp", None),
        P(("rep", "fsdp"), None, None),
        P(("rep", "fsdp"), None, None),
        P(("rep", "fsdp"), None, None),
        P(("rep", "fsdp"), None, None),
        P(),
    )
    out_specs = (
        P(("rep", "fsdp"), None, None),
        P(("rep", "fsdp"), None, None),
        P(None, ("rep", "fsdp"), None),
    )
    return jax.shard_map(body, mesh=mesh, in_specs=in_specs, out_specs=out_specs, check_vma=False)
```

time: 174 us -> 131 us (0.75)
  waiting for transfers between devices: 94.4 us -> 48.9 us
  blocking collectives: 0 us -> 41.7 us
  matrix products: 22.3 us -> 0 us
  Pallas kernels: 0 us -> 19 us
  between operations: 15.4 us -> 0.76 us
  other arithmetic: 11.5 us -> 0.33 us
  starting transfers between devices: 14.2 us -> 8.8 us
  local copies, waits for them, and re-layouts: 15.3 us -> 11.5 us
    unnamed x2 -> x0, waiting for transfers between devices: 47.5 us -> none
    all_to_all x0 -> x1, blocking collectives: none -> 41.7 us  [body(): lax.all_to_all(pieces, ('rep', 'fsdp'), split_axis=0, concat_axis=0, tile...]
    ppermute x0 -> x4, waiting for transfers between devices: none -> 31.2 us  [the longest x2 20.9 us: body(): arrived.append(lax.ppermute(packed, 'rep', orders[half][0]))]
    all_to_all x2 -> x1, waiting for transfers between devices: 46.9 us -> 17.7 us  [body(): lax.all_to_all(update_block.reshape(devices, size // devices, size), ('re...]
    dot_general x3 -> x0, matrix products: 22.3 us -> none  [the longest x1 9.52 us: precondition(): precond = jnp.dot(middle, right_root, preferred_element_type=jnp.float32)]
    pallas_call x0 -> x8, Pallas kernels: none -> 19 us  [the longest x1 6.69 us: statistics(): pl.pallas_call(statistics_kernel, grid=(strips,), out_shape=[jax.ShapeDty...]
    all_to_all x2 -> x1, starting transfers between devices: 14.2 us -> 4.7 us  [body(): lax.all_to_all(update_block.reshape(devices, size // devices, size), ('re...]
    gather x2 -> x0, local copies, waits for them, and re-layouts: 4.23 us -> none  [the longest x1 2.23 us: body(): returned_pieces = jnp.take(returned, owners, axis=0)]
  transfers between devices with their start and end apart: 3 -> 5, of which waited for: 3 -> 5; matrix products, arithmetic and copies ran while one was open for 7% -> 0% of each run, Pallas kernels for 0% -> 8%
where the time goes in v1:
time: 131 us
  waiting for transfers between devices  48.9 us (37%)
  blocking collectives  41.7 us (32%)
  Pallas kernels  19 us (15%)
  local copies, waits for them, and re-layouts  11.5 us (9%)
  starting transfers between devices  8.8 us (7%)
    all_to_all x1, blocking collectives, body(): lax.all_to_all(pieces, ('rep', 'fsdp'), split_axis=0, concat_axis=0, tile...  41.7 us
    ppermute x2, waiting for transfers between devices, body(): arrived.append(lax.ppermute(packed, 'rep', orders[half][0]))  20.9 us
    all_to_all x1, waiting for transfers between devices, body(): lax.all_to_all(update_block.reshape(devices, size // devices, size), ('re...  17.7 us
    unnamed x22, local copies, waits for them, and re-layouts  11.5 us
    ppermute x2, waiting for transfers between devices, body(): received.append(lax.ppermute(sending, 'rep', orders[half][1]))  10.3 us
    pallas_call x1, Pallas kernels, statistics(): pl.pallas_call(statistics_kernel, grid=(strips,), out_shape=[jax.ShapeDty...  6.69 us
    pallas_call x1, Pallas kernels, block_update(): pl.pallas_call(functools.partial(update_kernel, tiles=tiles), grid=(tiles...  5.41 us
    all_to_all x1, starting transfers between devices, body(): lax.all_to_all(update_block.reshape(devices, size // devices, size), ('re...  4.7 us
  transfers between devices with their start and end apart: 5, of which 5 were waited for; matrix products, arithmetic and copies ran while one was open for 0% of the time, Pallas kernels for 8%

profile of v1, /device:TPU:1, one launch (start us, length us, event | category | flops | bytes accessed | tf_op | source)
XLA Modules:
  0.0 131.0 jit_solution(6892900601683550482)
XLA Ops:
  0.6 0.1 pad_add_fusion.3.strips
  0.7 0.0 copy-start
  0.7 2.1 %copy-done = bf16[1,12,32,5120]{3,2,1,0:T(8,128)(2,1)S(1)} copy-done((bf16[1,12,32,5120]{3,2,1,0:T(8,128)(2,1)S(1)}, bf16[1,12,32,5120]{3,2,1,0:T(8,128)(2,1)}, u32[]{:S(2)}) %copy-start) | copy-done | bytes 3932184
  2.8 0.8 pack.3
  3.6 3.6 %collective-permute-start.2 = (bf16[2,5,6,32,256]{4,3,2,1,0:T(8,128)(2,1)S(1)}, bf16[2,5,6,32,256]{4,3,2,1,0:T(8,128)(2,1)S(1)}, u32[]{:S(2)}, u32[]{:S(2)}) collective-permute-start(bf16[2,5,6,32,256]{4,3,2,1,0:T(8,128)(2,1)S(1)} %pack.3), channel_id=1, source_target_pairs={{0,96},{32,64},{64,32},{96,0},{1,97},{33,65},{65,33},{97,1},{2,98}... | collective-permute-start | bytes 2949128 | tf_op jit(solution)/shard_map/ppermute | solution.py:241
  7.3 0.1 pad_add_fusion.1.strips
  7.4 0.0 copy-start.1
  7.4 2.1 %copy-done.1 = bf16[1,12,32,5120]{3,2,1,0:T(8,128)(2,1)S(1)} copy-done((bf16[1,12,32,5120]{3,2,1,0:T(8,128)(2,1)S(1)}, bf16[1,12,32,5120]{3,2,1,0:T(8,128)(2,1)}, u32[]{:S(2)}) %copy-start.1) | copy-done | bytes 3932184
  9.5 0.0 copy-start.2
  9.5 0.8 pack.2
  10.3 0.1 collective-permute-start
  10.4 0.1 pad_add_fusion
  10.5 18.2 %collective-permute-done.2.received = bf16[2,5,6,32,256]{4,3,2,1,0:T(8,128)(2,1)S(1)} collective-permute-done((bf16[2,5,6,32,256]{4,3,2,1,0:T(8,128)(2,1)S(1)}, bf16[2,5,6,32,256]{4,3,2,1,0:T(8,128)(2,1)S(1)}, u32[]{:S(2)}, u32[]{:S(2)}) %collective-permute-start.2) | collective-permute-done | bytes 983072 | tf_op jit(solution)/shard_map/ppermute | solution.py:241
  28.6 0.0 copy-done.2
  28.6 1.2 first_sum.3
  29.8 0.1 collective-permute-start.3
  29.9 2.8 %collective-permute-done.received = bf16[2,5,6,32,256]{4,3,2,1,0:T(8,128)(2,1)S(1)} collective-permute-done((bf16[2,5,6,32,256]{4,3,2,1,0:T(8,128)(2,1)S(1)}, bf16[2,5,6,32,256]{4,3,2,1,0:T(8,128)(2,1)S(1)}, u32[]{:S(2)}, u32[]{:S(2)}) %collective-permute-start) | collective-permute-done | bytes 983072 | tf_op jit(solution)/shard_map/ppermute | solution.py:241
  32.7 0.0 copy-start.10
  32.7 1.2 first_sum.2
  33.9 0.3 collective-permute-start.1
  34.2 0.0 copy-done.10
  34.2 0.1 select_reduce_fusion.owners
  34.3 8.9 %collective-permute-done.3.received_1 = bf16[5,6,32,256]{3,2,1,0:T(8,128)(2,1)S(1)} collective-permute-done((bf16[5,6,32,256]{3,2,1,0:T(8,128)(2,1)S(1)}, bf16[5,6,32,256]{3,2,1,0:T(8,128)(2,1)S(1)}, u32[]{:S(2)}, u32[]{:S(2)}) %collective-permute-start.3) | collective-permute-done | bytes 491552 | tf_op jit(solution)/shard_map/ppermute | solution.py:246
  43.2 1.3 %collective-permute-done.1.received_0 = bf16[5,6,32,256]{3,2,1,0:T(8,128)(2,1)S(1)} collective-permute-done((bf16[5,6,32,256]{3,2,1,0:T(8,128)(2,1)S(1)}, bf16[5,6,32,256]{3,2,1,0:T(8,128)(2,1)S(1)}, u32[]{:S(2)}, u32[]{:S(2)}) %collective-permute-start.1) | collective-permute-done | bytes 491552 | tf_op jit(solution)/shard_map/ppermute | solution.py:246
  44.6 0.9 second_sum.1
  45.4 0.0 copy-start.8
  45.5 0.0 copy-start.9
  45.5 41.7 %all_to_all.10 = bf16[128,32,256]{2,1,0:T(8,128)(2,1)S(1)} all-to-all(bf16[128,32,256]{2,1,0:T(8,128)(2,1)S(1)} %second_sum.1), channel_id=1, replica_groups=mesh['rep'=4,'fsdp'=32] {'rep','fsdp'}, dimensions={0} | all-to-all | bytes 4194304 | tf_op jit(solution)/shard_map/all_to_all | solution.py:248
  87.1 0.0 copy-start.3
  87.1 0.0 copy-done.8
  87.1 0.0 copy-done.9
  87.1 5.4 %block_update.1 = bf16[1024,1024]{1,0:T(8,128)(2,1)S(1)} custom-call(bf16[1,1024,1024]{2,1,0:T(8,128)(2,1)S(1)} %copy-done.8, bf16[4,1024,256]{2,1,0:T(8,128)(2,1)S(1)} %bitcast.7, bf16[1,1024,1024]{2,1,0:T(8,128)(2,1)S(1)} %copy-done.9), custom_call_target="tpu_custom_call" | custom-call | flops 4294967296 | bytes 8388608 | tf_op jit(solution)/shard_map/block_update/pallas_call | solution.py:137
  92.6 0.0 copy-done.3
  92.6 0.0 copy-start.5
  92.6 1.3 %copy-done.5 = bf16[1024,1024]{1,0:T(8,128)(2,1)} copy-done((bf16[1024,1024]{1,0:T(8,128)(2,1)}, bf16[1024,1024]{1,0:T(8,128)(2,1)S(1)}, u32[]{:S(2)}) %copy-start.5) | copy-done | bytes 2097176
  93.9 4.7 %all-to-all-start.1 = ((bf16[128,8,1024]{2,1,0:T(8,128)(2,1)}), bf16[128,8,1024]{2,1,0:T(8,128)(2,1)S(1)}, u32[]{:S(2)}, u32[]{:S(2)}) async-start(bf16[128,8,1024]{2,1,0:T(8,128)(2,1)} %bitcast.9), calls=%async_computation.1 | async-start | bytes 4194304 | tf_op jit(solution)/shard_map/all_to_all | solution.py:251
  98.6 0.0 copy-start.4
  98.6 1.6 %copy-done.4 = bf16[128,32,256]{2,1,0:T(8,128)(2,1)S(1)} copy-done((bf16[128,32,256]{2,1,0:T(8,128)(2,1)S(1)}, bf16[128,32,256]{2,1,0:T(8,128)(2,1)}, u32[]{:S(2)}) %copy-start.4) | copy-done | bytes 2097176
  100.2 0.0 copy-start.6
  100.2 2.2 %copy-done.6 = f32[1,1024,1024]{2,1,0:T(8,128)S(1)} copy-done((f32[1,1024,1024]{2,1,0:T(8,128)S(1)}, f32[1,1024,1024]{2,1,0:T(8,128)}, u32[]{:S(2)}) %copy-start.6) | copy-done | bytes 4194328
  102.4 0.0 copy-start.7
  102.4 2.2 %copy-done.7 = f32[1,1024,1024]{2,1,0:T(8,128)S(1)} copy-done((f32[1,1024,1024]{2,1,0:T(8,128)S(1)}, f32[1,1024,1024]{2,1,0:T(8,128)}, u32[]{:S(2)}) %copy-start.7) | copy-done | bytes 4194328
  104.6 6.7 %statistics.1 = (f32[1,1024,1024]{2,1,0:T(8,128)}, f32[1,1024,1024]{2,1,0:T(8,128)}) custom-call(bf16[4,1024,256]{2,1,0:T(8,128)(2,1)S(1)} %bitcast.8, f32[1,1024,1024]{2,1,0:T(8,128)S(1)} %copy-done.6, f32[1,1024,1024]{2,1,0:T(8,128)S(1)} %copy-done.7), custom_call_target="tpu_custom_call" | custom-call | flops 4294967296 | bytes 18874368 | tf_op jit(solution)/shard_map/statistics/pallas_call | solution.py:175
  111.3 17.7 %all-to-all-done.1.returned = bf16[128,8,1024]{2,1,0:T(8,128)(2,1)S(1)} async-done(((bf16[128,8,1024]{2,1,0:T(8,128)(2,1)}), bf16[128,8,1024]{2,1,0:T(8,128)(2,1)S(1)}, u32[]{:S(2)}, u32[]{:S(2)}) %all-to-all-start.1) | async-done | bytes 2097184 | tf_op jit(solution)/shard_map/all_to_all | solution.py:251
  129.0 2.0 %pick.1 = bf16[12,8,5120]{2,1,0:T(8,128)(2,1)} custom-call(s32[60]{0:T(128)S(1)} %select_reduce_fusion.owners, bf16[128,8,1024]{2,1,0:T(8,128)(2,1)S(1)} %all-to-all-done.1.returned), custom_call_target="tpu_custom_call" | custom-call | tf_op jit(solution)/shard_map/pick/pallas_call | solution.py:208
Async XLA Ops:
  0.7 2.1 %copy-start = (bf16[1,12,32,5120]{3,2,1,0:T(8,128)(2,1)S(1)}, bf16[1,12,32,5120]{3,2,1,0:T(8,128)(2,1)}, u32[]{:S(2)}) copy-start(bf16[1,12,32,5120]{3,2,1,0:T(8,128)(2,1)} %passing.3) | copy-start | bytes 11796484
  3.6 25.0 %collective-permute-start.2 = (bf16[2,5,6,32,256]{4,3,2,1,0:T(8,128)(2,1)S(1)}, bf16[2,5,6,32,256]{4,3,2,1,0:T(8,128)(2,1)S(1)}, u32[]{:S(2)}, u32[]{:S(2)}) collective-permute-start(bf16[2,5,6,32,256]{4,3,2,1,0:T(8,128)(2,1)S(1)} %pack.3), channel_id=1, source_target_pairs={{0,96},{32,64},{64,32},{96,0},{1,97},{33,65},{65,33},{97,1},{2,98}... | collective-permute-start | bytes 2949128 | tf_op jit(solution)/shard_map/ppermute | solution.py:241
  7.4 2.1 %copy-start.1 = (bf16[1,12,32,5120]{3,2,1,0:T(8,128)(2,1)S(1)}, bf16[1,12,32,5120]{3,2,1,0:T(8,128)(2,1)}, u32[]{:S(2)}) copy-start(bf16[1,12,32,5120]{3,2,1,0:T(8,128)(2,1)} %passing.3) | copy-start | bytes 11796484
  9.5 19.1 %copy-start.2 = (bf16[1,12,32,5120]{3,2,1,0:T(8,128)(2,1)S(1)}, bf16[1,12,32,5120]{3,2,1,0:T(8,128)(2,1)}, u32[]{:S(2)}) copy-start(bf16[1,12,32,5120]{3,2,1,0:T(8,128)(2,1)} %passing.3) | copy-start | bytes 11796484
  10.3 22.4 %collective-permute-start = (bf16[2,5,6,32,256]{4,3,2,1,0:T(8,128)(2,1)S(1)}, bf16[2,5,6,32,256]{4,3,2,1,0:T(8,128)(2,1)S(1)}, u32[]{:S(2)}, u32[]{:S(2)}) collective-permute-start(bf16[2,5,6,32,256]{4,3,2,1,0:T(8,128)(2,1)S(1)} %pack.2), channel_id=1, source_target_pairs={{0,32},{32,0},{64,96},{96,64},{1,33},{33,1},{65,97},{97,65},{2,34}... | collective-permute-start | bytes 2949128 | tf_op jit(solution)/shard_map/ppermute | solution.py:241
  29.8 13.4 %collective-permute-start.3 = (bf16[5,6,32,256]{3,2,1,0:T(8,128)(2,1)S(1)}, bf16[5,6,32,256]{3,2,1,0:T(8,128)(2,1)S(1)}, u32[]{:S(2)}, u32[]{:S(2)}) collective-permute-start(bf16[5,6,32,256]{3,2,1,0:T(8,128)(2,1)S(1)} %get-tuple-element.12), channel_id=1, source_target_pairs={{0,32},{32,0},{64,96},{96,64},{1,33},{33,1},{65,97},{97,65},{2,34}... | collective-permute-start | bytes 1474568 | tf_op jit(solution)/shard_map/ppermute | solution.py:246
  32.7 1.5 %copy-start.10 = (s32[128]{0:T(128)S(1)}, s32[128]{0:T(128)}, u32[]{:S(2)}) copy-start(s32[128]{0:T(128)} %param.11) | copy-start | bytes 1540
  33.9 10.7 %collective-permute-start.1 = (bf16[5,6,32,256]{3,2,1,0:T(8,128)(2,1)S(1)}, bf16[5,6,32,256]{3,2,1,0:T(8,128)(2,1)S(1)}, u32[]{:S(2)}, u32[]{:S(2)}) collective-permute-start(bf16[5,6,32,256]{3,2,1,0:T(8,128)(2,1)S(1)} %get-tuple-element.10), channel_id=1, source_target_pairs={{0,96},{32,64},{64,32},{96,0},{1,97},{33,65},{65,33},{97,1},{2,98}... | collective-permute-start | bytes 1474568 | tf_op jit(solution)/shard_map/ppermute | solution.py:246
  45.4 41.7 %copy-start.8 = (bf16[1,1024,1024]{2,1,0:T(8,128)(2,1)S(1)}, bf16[1,1024,1024]{2,1,0:T(8,128)(2,1)}, u32[]{:S(2)}) copy-start(bf16[1,1024,1024]{2,1,0:T(8,128)(2,1)} %left.3) | copy-start | bytes 6291460
  45.5 41.7 %copy-start.9 = (bf16[1,1024,1024]{2,1,0:T(8,128)(2,1)S(1)}, bf16[1,1024,1024]{2,1,0:T(8,128)(2,1)}, u32[]{:S(2)}) copy-start(bf16[1,1024,1024]{2,1,0:T(8,128)(2,1)} %right.3) | copy-start | bytes 6291460
  87.1 5.4 %copy-start.3 = (bf16[128,32,256]{2,1,0:T(8,128)(2,1)}, bf16[128,32,256]{2,1,0:T(8,128)(2,1)S(1)}, u32[]{:S(2)}) copy-start(bf16[128,32,256]{2,1,0:T(8,128)(2,1)S(1)} %all_to_all.10) | copy-start | bytes 6291460
  92.6 1.3 %copy-start.5 = (bf16[1024,1024]{1,0:T(8,128)(2,1)}, bf16[1024,1024]{1,0:T(8,128)(2,1)S(1)}, u32[]{:S(2)}) copy-start(bf16[1024,1024]{1,0:T(8,128)(2,1)S(1)} %block_update.1) | copy-start | bytes 6291460
  93.9 35.1 %all-to-all-start.1 = ((bf16[128,8,1024]{2,1,0:T(8,128)(2,1)}), bf16[128,8,1024]{2,1,0:T(8,128)(2,1)S(1)}, u32[]{:S(2)}, u32[]{:S(2)}) async-start(bf16[128,8,1024]{2,1,0:T(8,128)(2,1)} %bitcast.9), calls=%async_computation.1 | async-start | bytes 4194304 | tf_op jit(solution)/shard_map/all_to_all | solution.py:251
  98.6 1.6 %copy-start.4 = (bf16[128,32,256]{2,1,0:T(8,128)(2,1)S(1)}, bf16[128,32,256]{2,1,0:T(8,128)(2,1)}, u32[]{:S(2)}) copy-start(bf16[128,32,256]{2,1,0:T(8,128)(2,1)} %copy-done.3) | copy-start | bytes 6291460
  100.2 2.2 %copy-start.6 = (f32[1,1024,1024]{2,1,0:T(8,128)S(1)}, f32[1,1024,1024]{2,1,0:T(8,128)}, u32[]{:S(2)}) copy-start(f32[1,1024,1024]{2,1,0:T(8,128)} %left.2) | copy-start | bytes 12582916
  102.4 2.2 %copy-start.7 = (f32[1,1024,1024]{2,1,0:T(8,128)S(1)}, f32[1,1024,1024]{2,1,0:T(8,128)}, u32[]{:S(2)}) copy-start(f32[1,1024,1024]{2,1,0:T(8,128)} %right.2) | copy-start | bytes 12582916

commit v2 on v1

v2 whole, which is shorter than its diff:
```python
import functools

import jax
import jax.numpy as jnp
from jax import lax
from jax.experimental import pallas as pl
from jax.experimental.pallas import tpu as pltpu
from jax.sharding import PartitionSpec as P

DECAY = 0.95
EPSILON = 1e-06
MIB = 1 << 20


def params(mib):
    return pltpu.CompilerParams(vmem_limit_bytes=mib * MIB)


def first_partner(part, me, reps):
    return (me ^ 1, reps - 1 - me)[part % 2]


def second_partner(part, me, reps):
    return (reps - 1 - me, me ^ 1)[part % 2]


def pack_kernel(grads, *rest, parts, own, groups, columns, reps, width):
    outs, sem = rest[:-1], rest[-1]
    me = lax.axis_index("rep")
    copies = []
    for out, part in zip(outs, parts):
        target = me if own else first_partner(part, me, reps)
        for which, strip in enumerate((target, second_partner(part, target, reps))):
            for column in range(columns):
                offset = pl.multiple_of((column * reps + strip) * width, width)
                copies.append(
                    pltpu.make_async_copy(
                        grads.at[0, pl.ds(part * groups, groups), :, pl.ds(offset, width)],
                        out.at[which, column],
                        sem.at[len(copies)],
                    )
                )
    for copy in copies:
        copy.start()
    for copy in copies:
        copy.wait()


def pack(grads, parts, own, groups, columns, reps, width):
    shape = jax.ShapeDtypeStruct((2, columns, groups, grads.shape[2], width), grads.dtype)
    return pl.pallas_call(
        functools.partial(
            pack_kernel, parts=parts, own=own, groups=groups, columns=columns, reps=reps, width=width
        ),
        out_shape=[shape] * len(parts),
        in_specs=[pl.BlockSpec(memory_space=pltpu.HBM)],
        out_specs=[pl.BlockSpec(memory_space=pl.ANY)] * len(parts),
        scratch_shapes=[pltpu.SemaphoreType.DMA((2 * columns * len(parts),))],
        compiler_params=params(16),
        name="pack_own" if own else "pack",
    )(pltpu.with_memory_space_constraint(grads, pltpu.HBM))


def first_sum_kernel(own, received, sending):
    _, columns, groups, _, _ = own.shape
    for column in range(columns):
        for group in range(groups):
            total = own[1, column, group].astype(jnp.float32) + received[1, column, group].astype(jnp.float32)
            sending[column, group] = total.astype(sending.dtype)


def first_sum(own, received):
    return pl.pallas_call(
        first_sum_kernel,
        out_shape=jax.ShapeDtypeStruct(own.shape[1:], own.dtype),
        in_specs=[pl.BlockSpec(memory_space=pltpu.VMEM)] * 2,
        out_specs=pl.BlockSpec(memory_space=pltpu.VMEM),
        compiler_params=params(16),
        name="first_sum",
    )(own, received)


def second_sum_kernel(owners, *refs, parts, columns, groups, initial):
    out = refs[-1]
    if initial:
        out[...] = jnp.zeros_like(out)
    for index, part in enumerate(parts):
        own, first, second = refs[3 * index : 3 * index + 3]
        for group in range(groups):
            for column in range(columns):
                owner = owners[(part * groups + group) * columns + column]
                total = own[0, column, group].astype(jnp.float32) + first[0, column, group].astype(jnp.float32)
                total += second[column, group].astype(jnp.float32)
                out[owner] = total.astype(out.dtype)


def second_sum(owners, terms, parts, devices, before=None):
    _, columns, groups, height, width = terms[0][0].shape
    arrays = [array for part in parts for array in terms[part]]
    aliases = {}
    if before is not None:
        arrays.append(before)
        aliases = {len(arrays): 0}
    return pl.pallas_call(
        functools.partial(
            second_sum_kernel, parts=parts, columns=columns, groups=groups, initial=before is None
        ),
        out_shape=jax.ShapeDtypeStruct((devices, height, width), arrays[0].dtype),
        in_specs=[pl.BlockSpec(memory_space=pltpu.SMEM)] + [pl.BlockSpec(memory_space=pltpu.VMEM)] * len(arrays),
        out_specs=pl.BlockSpec(memory_space=pltpu.VMEM),
        input_output_aliases=aliases,
        compiler_params=params(16),
        name="second_sum",
    )(owners, *arrays)


def update_kernel(left, grad, right, out, precond, scaled, sem, *, tiles, out_tiles):
    strips, size, width = grad.shape
    rows = size // tiles
    grad_square = jnp.zeros((8, width), jnp.float32)
    square = jnp.zeros((8, size), jnp.float32)
    for tile in range(tiles):
        band = slice(tile * rows, (tile + 1) * rows)
        middle = jnp.concatenate(
            [
                jnp.dot(left[0, band, :], grad[strip], preferred_element_type=jnp.float32).astype(jnp.bfloat16)
                for strip in range(strips)
            ],
            axis=1,
        )
        for strip in range(tile * strips // tiles, (tile + 1) * strips // tiles):
            as_float = grad[strip].astype(jnp.float32)
            grad_square += jnp.sum((as_float * as_float).reshape(size // 8, 8, width), axis=0)
        part = jnp.dot(middle, right[0], preferred_element_type=jnp.float32)
        precond[band, :] = part
        square += jnp.sum((part * part).reshape(rows // 8, 8, size), axis=0)
    entries = size * size
    mean_grad = jnp.full((8, 128), jnp.sum(grad_square) / entries)
    mean_precond = jnp.full((8, 128), jnp.sum(square) / entries)
    scale = jnp.sqrt(mean_grad / (mean_precond + EPSILON))[0:1, 0:1]
    out_rows = size // out_tiles
    copies = []
    for tile in range(out_tiles):
        band = slice(tile * out_rows, (tile + 1) * out_rows)
        scaled[band, :] = (precond[band, :] * scale).astype(out.dtype)
        copies.append(pltpu.make_async_copy(scaled.at[band, :], out.at[band, :], sem.at[tile]))
        copies[-1].start()
    for copy in copies:
        copy.wait()


def block_update(left, grad, right, tiles=2, out_tiles=4):
    strips, size, width = grad.shape
    return pl.pallas_call(
        functools.partial(update_kernel, tiles=tiles, out_tiles=out_tiles),
        out_shape=pltpu.HBM((size, size), jnp.bfloat16),
        in_specs=[pl.BlockSpec(memory_space=pltpu.VMEM)] * 3,
        out_specs=pl.BlockSpec(memory_space=pltpu.HBM),
        scratch_shapes=[
            pltpu.VMEM((size, size), jnp.float32),
            pltpu.VMEM((size, size), jnp.bfloat16),
            pltpu.SemaphoreType.DMA((out_tiles,)),
        ],
        compiler_params=params(32),
        cost_estimate=pl.CostEstimate(flops=4 * size**3, bytes_accessed=8 * size * size, transcendentals=0),
        name="block_update",
    )(left, grad, right)


def statistics_kernel(grad, left, right, new_left, new_right):
    step = pl.program_id(0)
    strips, size, width = grad.shape
    rows = pl.ds(pl.multiple_of(step * width, width), width)
    gram = jnp.zeros((width, size), jnp.float32)
    for strip in range(strips):
        gram += lax.dot_general(
            grad[strip, rows, :], grad[strip], (((1,), (1,)), ((), ())), preferred_element_type=jnp.float32
        )
    new_left[0] = DECAY * left[0] + (1.0 - DECAY) * gram
    for strip in range(strips):
        columns = slice(strip * width, (strip + 1) * width)
        gram = lax.dot_general(
            grad[step], grad[strip], (((0,), (0,)), ((), ())), preferred_element_type=jnp.float32
        )
        new_right[0, :, columns] = DECAY * right[0, :, columns] + (1.0 - DECAY) * gram


def statistics(grad, left, right):
    strips, size, width = grad.shape
    rows = pl.BlockSpec((1, width, size), lambda t: (0, t, 0))
    return pl.pallas_call(
        statistics_kernel,
        grid=(strips,),
        out_shape=[jax.ShapeDtypeStruct(left.shape, left.dtype)] * 2,
        in_specs=[pl.BlockSpec((strips, size, width), lambda t: (0, 0, 0)), rows, rows],
        out_specs=[rows, rows],
        compiler_params=params(32),
        cost_estimate=pl.CostEstimate(flops=4 * size**3, bytes_accessed=18 * size * size, transcendentals=0),
        name="statistics",
    )(grad, left, right)


def pick_kernel(owners, returned, out, sem, *, columns, size):
    groups = out.shape[0]
    copies = []
    for group in range(groups):
        for column in range(columns):
            block = group * columns + column
            copies.append(
                pltpu.make_async_copy(
                    returned.at[owners[block]],
                    out.at[group, :, pl.ds(column * size, size)],
                    sem.at[block],
                )
            )
    for copy in copies:
        copy.start()
    for copy in copies:
        copy.wait()


def pick(owners, returned, groups, columns):
    _, rows, size = returned.shape
    return pl.pallas_call(
        functools.partial(pick_kernel, columns=columns, size=size),
        out_shape=jax.ShapeDtypeStruct((groups, rows, columns * size), returned.dtype),
        in_specs=[pl.BlockSpec(memory_space=pltpu.SMEM), pl.BlockSpec(memory_space=pl.ANY)],
        out_specs=pl.BlockSpec(memory_space=pl.ANY),
        scratch_shapes=[pltpu.SemaphoreType.DMA((groups * columns,))],
        compiler_params=params(16),
        name="pick",
    )(owners, returned)


def body(grads, stat_left, stat_right, root_left, root_right, owner_block):
    reps = lax.axis_size("rep")
    devices = lax.axis_size("fsdp") * reps
    size = stat_left.shape[1]
    groups, full_width = grads.shape[1], grads.shape[3]
    columns = full_width // size
    width = size // reps
    across = [(r, r ^ 1) for r in range(reps)]
    mirror = [(r, reps - 1 - r) for r in range(reps)]
    orders = ((across, mirror), (mirror, across))

    matches = owner_block[None, :] == lax.iota(jnp.int32, groups * columns)[:, None]
    owners = jnp.sum(jnp.where(matches, lax.iota(jnp.int32, devices)[None, :], 0), axis=1)

    parts = 4
    part_groups = groups // parts
    sizes = (part_groups, columns, reps, width)
    packed = pack(grads, (0, 1), False, *sizes) + pack(grads, (2, 3), False, *sizes)
    firsts = [lax.ppermute(packed[part], "rep", orders[part % 2][0]) for part in range(parts)]
    own = pack(grads, tuple(range(parts)), True, *sizes)
    seconds = [
        lax.ppermute(first_sum(own[part], firsts[part]), "rep", orders[part % 2][1]) for part in range(parts)
    ]
    terms = list(zip(own, firsts, seconds))
    pieces = second_sum(owners, terms, (0, 1), devices)
    pieces = second_sum(owners, terms, (2, 3), devices, pieces)
    grad_block = lax.all_to_all(pieces, ("rep", "fsdp"), split_axis=0, concat_axis=0, tiled=True)
    grad_block = grad_block.reshape(reps, size, width)
    update_block = block_update(root_left, grad_block, root_right)
    returned = lax.all_to_all(
        update_block.reshape(devices, size // devices, size),
        ("rep", "fsdp"),
        split_axis=0,
        concat_axis=0,
        tiled=True,
    )
    new_left, new_right = statistics(grad_block, stat_left, stat_right)
    return (new_left, new_right, pick(owners, returned, groups, columns))


def solution(mesh):
    in_specs = (
        P("rep", None, "fsdp", None),
        P(("rep", "fsdp"), None, None),
        P(("rep", "fsdp"), None, None),
        P(("rep", "fsdp"), None, None),
        P(("rep", "fsdp"), None, None),
        P(),
    )
    out_specs = (
        P(("rep", "fsdp"), None, None),
        P(("rep", "fsdp"), None, None),
        P(None, ("rep", "fsdp"), None),
    )
    return jax.shard_map(body, mesh=mesh, in_specs=in_specs, out_specs=out_specs, check_vma=False)
```

time: 131 us -> 124 us (0.947)
  waiting for transfers between devices: 48.9 us -> 40.7 us
  local copies, waits for them, and re-layouts: 11.5 us -> 5.98 us
  starting transfers between devices: 8.8 us -> 13.7 us
  Pallas kernels: 19 us -> 21.5 us
  blocking collectives: 41.7 us -> 40.2 us
    ppermute x4 -> x8, waiting for transfers between devices: 31.2 us -> 23 us  [the longest x4 15.2 us: body(): lax.ppermute(packed[part], 'rep', orders[part % 2][0])]
    unnamed x22 -> x14, local copies, waits for them, and re-layouts: 11.5 us -> 5.98 us
    ppermute x4 -> x8, starting transfers between devices: 4.09 us -> 9.02 us  [the longest x4 5.28 us: body(): lax.ppermute(packed[part], 'rep', orders[part % 2][0])]
    pallas_call x6 -> x10, Pallas kernels: 10.3 us -> 12.8 us  [the longest x1 6.35 us: block_update(): pl.pallas_call(functools.partial(update_kernel, tiles=tiles, out_tiles=ou...]
    all_to_all x1, blocking collectives: 41.7 us -> 40.2 us  [body(): lax.all_to_all(pieces, ('rep', 'fsdp'), split_axis=0, concat_axis=0, tile...]
  transfers between devices with their start and end apart: 5 -> 9, of which waited for: 5 -> 7; matrix products, arithmetic and copies ran while one was open for 0% -> 0% of each run, Pallas kernels for 8% -> 9%
where the time goes in v2:
time: 124 us; the launch traced here: 123 us
  waiting for transfers between devices  40.7 us (33%)
  blocking collectives  40.2 us (32%)
  Pallas kernels  21.5 us (17%)
  starting transfers between devices  13.7 us (11%)
  local copies, waits for them, and re-layouts  5.98 us (5%)
    all_to_all x1, blocking collectives, body(): lax.all_to_all(pieces, ('rep', 'fsdp'), split_axis=0, concat_axis=0, tile...  40.2 us
    all_to_all x1, waiting for transfers between devices, body(): lax.all_to_all(update_block.reshape(devices, size // devices, size), ('re...  17.7 us
    ppermute x4, waiting for transfers between devices, body(): lax.ppermute(packed[part], 'rep', orders[part % 2][0])  15.2 us
    ppermute x4, waiting for transfers between devices, body(): lax.ppermute(first_sum(own[part], firsts[part]), 'rep', orders[part % 2][1])  7.74 us
    pallas_call x1, Pallas kernels, statistics(): pl.pallas_call(statistics_kernel, grid=(strips,), out_shape=[jax.ShapeDty...  6.7 us
    pallas_call x1, Pallas kernels, block_update(): pl.pallas_call(functools.partial(update_kernel, tiles=tiles, out_tiles=ou...  6.35 us
    unnamed x14, local copies, waits for them, and re-layouts  5.98 us
    ppermute x4, starting transfers between devices, body(): lax.ppermute(packed[part], 'rep', orders[part % 2][0])  5.28 us
  transfers between devices with their start and end apart: 9, of which 7 were waited for; matrix products, arithmetic and copies ran while one was open for 0% of the time, Pallas kernels for 9%

profile of v2, /device:TPU:1, one launch (start us, length us, event | category | flops | bytes accessed | tf_op | source)
XLA Modules:
  0.0 122.9 jit_solution(15970479353491023723)
XLA Ops:
  0.6 1.4 %pack.3 = (bf16[2,5,3,32,256]{4,3,2,1,0:T(8,128)(2,1)S(1)}, bf16[2,5,3,32,256]{4,3,2,1,0:T(8,128)(2,1)S(1)}) custom-call(bf16[1,12,32,5120]{3,2,1,0:T(8,128)(2,1)} %grads.5), custom_call_target="tpu_custom_call" | custom-call | tf_op jit(solution)/shard_map/pack/pallas_call | solution.py:51
  2.0 3.6 %collective-permute-start.6 = (bf16[2,5,3,32,256]{4,3,2,1,0:T(8,128)(2,1)S(1)}, bf16[2,5,3,32,256]{4,3,2,1,0:T(8,128)(2,1)S(1)}, u32[]{:S(2)}, u32[]{:S(2)}) collective-permute-start(bf16[2,5,3,32,256]{4,3,2,1,0:T(8,128)(2,1)S(1)} %get-tuple-element.20), channel_id=1, source_target_pairs={{0,96},{32,64},{64,32},{96,0},{1,97},{33,65},{65,33},{97,1},{2,98}... | collective-permute-start | bytes 1474568 | tf_op jit(solution)/shard_map/ppermute | solution.py:253
  5.7 0.0 collective-permute-start.4
  5.7 1.4 %pack.2 = (bf16[2,5,3,32,256]{4,3,2,1,0:T(8,128)(2,1)S(1)}, bf16[2,5,3,32,256]{4,3,2,1,0:T(8,128)(2,1)S(1)}) custom-call(bf16[1,12,32,5120]{3,2,1,0:T(8,128)(2,1)} %grads.5), custom_call_target="tpu_custom_call" | custom-call | tf_op jit(solution)/shard_map/pack/pallas_call | solution.py:51
  7.1 0.7 collective-permute-start.2
  7.8 0.9 collective-permute-start
  8.7 1.9 %pack_own.1 = (bf16[2,5,3,32,256]{4,3,2,1,0:T(8,128)(2,1)S(1)}, bf16[2,5,3,32,256]{4,3,2,1,0:T(8,128)(2,1)S(1)}, bf16[2,5,3,32,256]{4,3,2,1,0:T(8,128)(2,1)S(1)}, bf16[2,5,3,32,256]{4,3,2,1,0:T(8,128)(2,1)S(1)}) custom-call(bf16[1,12,32,5120]{3,2,1,0:T(8,128)(2,1)} %grads.5), custom_call_target="tpu_custom_call" | custom-call | tf_op jit(solution)/shard_map/pack_own/pallas_call | solution.py:51
  10.6 5.9 %collective-permute-done.6.received.refs_4_ = bf16[2,5,3,32,256]{4,3,2,1,0:T(8,128)(2,1)S(1)} collective-permute-done((bf16[2,5,3,32,256]{4,3,2,1,0:T(8,128)(2,1)S(1)}, bf16[2,5,3,32,256]{4,3,2,1,0:T(8,128)(2,1)S(1)}, u32[]{:S(2)}, u32[]{:S(2)}) %collective-permute-start.6) | collective-permute-done | bytes 491552 | tf_op jit(solution)/shard_map/ppermute | solution.py:253
  16.5 0.1 first_sum.7
  16.5 0.0 copy-start.6
  16.5 0.1 collective-permute-start.7
  16.6 0.8 collective-permute-done.4.received.refs_1_
  17.4 0.1 first_sum.6
  17.5 1.8 %collective-permute-start.5 = (bf16[5,3,32,256]{3,2,1,0:T(8,128)(2,1)S(1)}, bf16[5,3,32,256]{3,2,1,0:T(8,128)(2,1)S(1)}, u32[]{:S(2)}, u32[]{:S(2)}) collective-permute-start(bf16[5,3,32,256]{3,2,1,0:T(8,128)(2,1)S(1)} %first_sum.6), channel_id=1, source_target_pairs={{0,96},{32,64},{64,32},{96,0},{1,97},{33,65},{65,33},{97,1},{2,98}... | collective-permute-start | bytes 737288 | tf_op jit(solution)/shard_map/ppermute | solution.py:256
  19.3 7.7 %collective-permute-done.2.received.refs_4_ = bf16[2,5,3,32,256]{4,3,2,1,0:T(8,128)(2,1)S(1)} collective-permute-done((bf16[2,5,3,32,256]{4,3,2,1,0:T(8,128)(2,1)S(1)}, bf16[2,5,3,32,256]{4,3,2,1,0:T(8,128)(2,1)S(1)}, u32[]{:S(2)}, u32[]{:S(2)}) %collective-permute-start.2) | collective-permute-done | bytes 491552 | tf_op jit(solution)/shard_map/ppermute | solution.py:253
  27.0 0.1 first_sum.5
  27.1 0.1 collective-permute-start.3
  27.2 0.8 collective-permute-done.received.refs_1_
  28.0 0.1 first_sum.4
  28.0 1.8 %collective-permute-start.1 = (bf16[5,3,32,256]{3,2,1,0:T(8,128)(2,1)S(1)}, bf16[5,3,32,256]{3,2,1,0:T(8,128)(2,1)S(1)}, u32[]{:S(2)}, u32[]{:S(2)}) collective-permute-start(bf16[5,3,32,256]{3,2,1,0:T(8,128)(2,1)S(1)} %first_sum.4), channel_id=1, source_target_pairs={{0,96},{32,64},{64,32},{96,0},{1,97},{33,65},{65,33},{97,1},{2,98}... | collective-permute-start | bytes 737288 | tf_op jit(solution)/shard_map/ppermute | solution.py:256
  29.8 0.0 copy-done.6
  29.8 0.1 select_reduce_fusion.owners
  29.9 3.3 %collective-permute-done.7.refs_5_ = bf16[5,3,32,256]{3,2,1,0:T(8,128)(2,1)S(1)} collective-permute-done((bf16[5,3,32,256]{3,2,1,0:T(8,128)(2,1)S(1)}, bf16[5,3,32,256]{3,2,1,0:T(8,128)(2,1)S(1)}, u32[]{:S(2)}, u32[]{:S(2)}) %collective-permute-start.7) | collective-permute-done | bytes 245792 | tf_op jit(solution)/shard_map/ppermute | solution.py:256
  33.2 0.0 collective-permute-done.5.refs_2_
  33.2 0.8 second_sum.2.refs_6_
  34.1 4.4 %collective-permute-done.3.refs_5_ = bf16[5,3,32,256]{3,2,1,0:T(8,128)(2,1)S(1)} collective-permute-done((bf16[5,3,32,256]{3,2,1,0:T(8,128)(2,1)S(1)}, bf16[5,3,32,256]{3,2,1,0:T(8,128)(2,1)S(1)}, u32[]{:S(2)}, u32[]{:S(2)}) %collective-permute-start.3) | collective-permute-done | bytes 245792 | tf_op jit(solution)/shard_map/ppermute | solution.py:256
  38.5 0.0 collective-permute-done.1.refs_2_
  38.5 0.7 second_sum.3
  39.2 0.0 copy-start.4
  39.3 0.0 copy-start.5
  39.3 40.2 %all_to_all.10 = bf16[128,32,256]{2,1,0:T(8,128)(2,1)S(1)} all-to-all(bf16[128,32,256]{2,1,0:T(8,128)(2,1)S(1)} %second_sum.3), channel_id=1, replica_groups=mesh['rep'=4,'fsdp'=32] {'rep','fsdp'}, dimensions={0} | all-to-all | bytes 4194304 | tf_op jit(solution)/shard_map/all_to_all | solution.py:261
  79.5 0.0 copy-start
  79.5 0.0 copy-done.4
  79.5 0.0 copy-done.5
  79.5 6.3 %block_update.1 = bf16[1024,1024]{1,0:T(8,128)(2,1)} custom-call(bf16[1,1024,1024]{2,1,0:T(8,128)(2,1)S(1)} %copy-done.4, bf16[4,1024,256]{2,1,0:T(8,128)(2,1)S(1)} %bitcast.2, bf16[1,1024,1024]{2,1,0:T(8,128)(2,1)S(1)} %copy-done.5), custom_call_target="tpu_custom_call" | custom-call | flops 4294967296 | bytes 8388608 | tf_op jit(solution)/shard_map/block_update/pallas_call | solution.py:154
  85.8 0.0 copy-done
  85.8 4.7 %all-to-all-start.1 = ((bf16[128,8,1024]{2,1,0:T(8,128)(2,1)}), bf16[128,8,1024]{2,1,0:T(8,128)(2,1)S(1)}, u32[]{:S(2)}, u32[]{:S(2)}) async-start(bf16[128,8,1024]{2,1,0:T(8,128)(2,1)} %bitcast.4), calls=%async_computation.1 | async-start | bytes 4194304 | tf_op jit(solution)/shard_map/all_to_all | solution.py:264
  90.6 0.0 copy-start.1
  90.6 1.6 %copy-done.1 = bf16[128,32,256]{2,1,0:T(8,128)(2,1)S(1)} copy-done((bf16[128,32,256]{2,1,0:T(8,128)(2,1)S(1)}, bf16[128,32,256]{2,1,0:T(8,128)(2,1)}, u32[]{:S(2)}) %copy-start.1) | copy-done | bytes 2097176
  92.2 0.0 copy-start.2
  92.2 2.2 %copy-done.2 = f32[1,1024,1024]{2,1,0:T(8,128)S(1)} copy-done((f32[1,1024,1024]{2,1,0:T(8,128)S(1)}, f32[1,1024,1024]{2,1,0:T(8,128)}, u32[]{:S(2)}) %copy-start.2) | copy-done | bytes 4194328
  94.3 0.0 copy-start.3
  94.4 2.2 %copy-done.3 = f32[1,1024,1024]{2,1,0:T(8,128)S(1)} copy-done((f32[1,1024,1024]{2,1,0:T(8,128)S(1)}, f32[1,1024,1024]{2,1,0:T(8,128)}, u32[]{:S(2)}) %copy-start.3) | copy-done | bytes 4194328
  96.5 6.7 %statistics.1 = (f32[1,1024,1024]{2,1,0:T(8,128)}, f32[1,1024,1024]{2,1,0:T(8,128)}) custom-call(bf16[4,1024,256]{2,1,0:T(8,128)(2,1)S(1)} %bitcast.3, f32[1,1024,1024]{2,1,0:T(8,128)S(1)} %copy-done.2, f32[1,1024,1024]{2,1,0:T(8,128)S(1)} %copy-done.3), custom_call_target="tpu_custom_call" | custom-call | flops 4294967296 | bytes 18874368 | tf_op jit(solution)/shard_map/statistics/pallas_call | solution.py:191
  103.2 17.7 %all-to-all-done.1.returned = bf16[128,8,1024]{2,1,0:T(8,128)(2,1)S(1)} async-done(((bf16[128,8,1024]{2,1,0:T(8,128)(2,1)}), bf16[128,8,1024]{2,1,0:T(8,128)(2,1)S(1)}, u32[]{:S(2)}, u32[]{:S(2)}) %all-to-all-start.1) | async-done | bytes 2097184 | tf_op jit(solution)/shard_map/all_to_all | solution.py:264
  120.9 2.0 %pick.1 = bf16[12,8,5120]{2,1,0:T(8,128)(2,1)} custom-call(s32[60]{0:T(128)S(1)} %select_reduce_fusion.owners, bf16[128,8,1024]{2,1,0:T(8,128)(2,1)S(1)} %all-to-all-done.1.returned), custom_call_target="tpu_custom_call" | custom-call | tf_op jit(solution)/shard_map/pick/pallas_call | solution.py:224
Async XLA Ops:
  2.0 14.4 %collective-permute-start.6 = (bf16[2,5,3,32,256]{4,3,2,1,0:T(8,128)(2,1)S(1)}, bf16[2,5,3,32,256]{4,3,2,1,0:T(8,128)(2,1)S(1)}, u32[]{:S(2)}, u32[]{:S(2)}) collective-permute-start(bf16[2,5,3,32,256]{4,3,2,1,0:T(8,128)(2,1)S(1)} %get-tuple-element.20), channel_id=1, source_target_pairs={{0,96},{32,64},{64,32},{96,0},{1,97},{33,65},{65,33},{97,1},{2,98}... | collective-permute-start | bytes 1474568 | tf_op jit(solution)/shard_map/ppermute | solution.py:253
  5.7 11.8 %collective-permute-start.4 = (bf16[2,5,3,32,256]{4,3,2,1,0:T(8,128)(2,1)S(1)}, bf16[2,5,3,32,256]{4,3,2,1,0:T(8,128)(2,1)S(1)}, u32[]{:S(2)}, u32[]{:S(2)}) collective-permute-start(bf16[2,5,3,32,256]{4,3,2,1,0:T(8,128)(2,1)S(1)} %get-tuple-element.18), channel_id=1, source_target_pairs={{0,32},{32,0},{64,96},{96,64},{1,33},{33,1},{65,97},{97,65},{2,34}... | collective-permute-start | bytes 1474568 | tf_op jit(solution)/shard_map/ppermute | solution.py:253
  7.1 19.9 %collective-permute-start.2 = (bf16[2,5,3,32,256]{4,3,2,1,0:T(8,128)(2,1)S(1)}, bf16[2,5,3,32,256]{4,3,2,1,0:T(8,128)(2,1)S(1)}, u32[]{:S(2)}, u32[]{:S(2)}) collective-permute-start(bf16[2,5,3,32,256]{4,3,2,1,0:T(8,128)(2,1)S(1)} %get-tuple-element.16), channel_id=1, source_target_pairs={{0,96},{32,64},{64,32},{96,0},{1,97},{33,65},{65,33},{97,1},{2,98}... | collective-permute-start | bytes 1474568 | tf_op jit(solution)/shard_map/ppermute | solution.py:253
  7.8 20.2 %collective-permute-start = (bf16[2,5,3,32,256]{4,3,2,1,0:T(8,128)(2,1)S(1)}, bf16[2,5,3,32,256]{4,3,2,1,0:T(8,128)(2,1)S(1)}, u32[]{:S(2)}, u32[]{:S(2)}) collective-permute-start(bf16[2,5,3,32,256]{4,3,2,1,0:T(8,128)(2,1)S(1)} %get-tuple-element.14), channel_id=1, source_target_pairs={{0,32},{32,0},{64,96},{96,64},{1,33},{33,1},{65,97},{97,65},{2,34}... | collective-permute-start | bytes 1474568 | tf_op jit(solution)/shard_map/ppermute | solution.py:253
  16.5 13.3 %copy-start.6 = (s32[128]{0:T(128)S(1)}, s32[128]{0:T(128)}, u32[]{:S(2)}) copy-start(s32[128]{0:T(128)} %param.11) | copy-start | bytes 1540
  16.5 16.7 %collective-permute-start.7 = (bf16[5,3,32,256]{3,2,1,0:T(8,128)(2,1)S(1)}, bf16[5,3,32,256]{3,2,1,0:T(8,128)(2,1)S(1)}, u32[]{:S(2)}, u32[]{:S(2)}) collective-permute-start(bf16[5,3,32,256]{3,2,1,0:T(8,128)(2,1)S(1)} %first_sum.7), channel_id=1, source_target_pairs={{0,32},{32,0},{64,96},{96,64},{1,33},{33,1},{65,97},{97,65},{2,34}... | collective-permute-start | bytes 737288 | tf_op jit(solution)/shard_map/ppermute | solution.py:256
  17.5 15.7 %collective-permute-start.5 = (bf16[5,3,32,256]{3,2,1,0:T(8,128)(2,1)S(1)}, bf16[5,3,32,256]{3,2,1,0:T(8,128)(2,1)S(1)}, u32[]{:S(2)}, u32[]{:S(2)}) collective-permute-start(bf16[5,3,32,256]{3,2,1,0:T(8,128)(2,1)S(1)} %first_sum.6), channel_id=1, source_target_pairs={{0,96},{32,64},{64,32},{96,0},{1,97},{33,65},{65,33},{97,1},{2,98}... | collective-permute-start | bytes 737288 | tf_op jit(solution)/shard_map/ppermute | solution.py:256
  27.1 11.4 %collective-permute-start.3 = (bf16[5,3,32,256]{3,2,1,0:T(8,128)(2,1)S(1)}, bf16[5,3,32,256]{3,2,1,0:T(8,128)(2,1)S(1)}, u32[]{:S(2)}, u32[]{:S(2)}) collective-permute-start(bf16[5,3,32,256]{3,2,1,0:T(8,128)(2,1)S(1)} %first_sum.5), channel_id=1, source_target_pairs={{0,32},{32,0},{64,96},{96,64},{1,33},{33,1},{65,97},{97,65},{2,34}... | collective-permute-start | bytes 737288 | tf_op jit(solution)/shard_map/ppermute | solution.py:256
  28.0 10.5 %collective-permute-start.1 = (bf16[5,3,32,256]{3,2,1,0:T(8,128)(2,1)S(1)}, bf16[5,3,32,256]{3,2,1,0:T(8,128)(2,1)S(1)}, u32[]{:S(2)}, u32[]{:S(2)}) collective-permute-start(bf16[5,3,32,256]{3,2,1,0:T(8,128)(2,1)S(1)} %first_sum.4), channel_id=1, source_target_pairs={{0,96},{32,64},{64,32},{96,0},{1,97},{33,65},{65,33},{97,1},{2,98}... | collective-permute-start | bytes 737288 | tf_op jit(solution)/shard_map/ppermute | solution.py:256
  39.2 40.2 %copy-start.4 = (bf16[1,1024,1024]{2,1,0:T(8,128)(2,1)S(1)}, bf16[1,1024,1024]{2,1,0:T(8,128)(2,1)}, u32[]{:S(2)}) copy-start(bf16[1,1024,1024]{2,1,0:T(8,128)(2,1)} %left.3) | copy-start | bytes 6291460
  39.3 40.2 %copy-start.5 = (bf16[1,1024,1024]{2,1,0:T(8,128)(2,1)S(1)}, bf16[1,1024,1024]{2,1,0:T(8,128)(2,1)}, u32[]{:S(2)}) copy-start(bf16[1,1024,1024]{2,1,0:T(8,128)(2,1)} %right.3) | copy-start | bytes 6291460
  79.5 6.4 %copy-start = (bf16[128,32,256]{2,1,0:T(8,128)(2,1)}, bf16[128,32,256]{2,1,0:T(8,128)(2,1)S(1)}, u32[]{:S(2)}) copy-start(bf16[128,32,256]{2,1,0:T(8,128)(2,1)S(1)} %all_to_all.10) | copy-start | bytes 6291460
  85.8 35.1 %all-to-all-start.1 = ((bf16[128,8,1024]{2,1,0:T(8,128)(2,1)}), bf16[128,8,1024]{2,1,0:T(8,128)(2,1)S(1)}, u32[]{:S(2)}, u32[]{:S(2)}) async-start(bf16[128,8,1024]{2,1,0:T(8,128)(2,1)} %bitcast.4), calls=%async_computation.1 | async-start | bytes 4194304 | tf_op jit(solution)/shard_map/all_to_all | solution.py:264
  90.6 1.6 %copy-start.1 = (bf16[128,32,256]{2,1,0:T(8,128)(2,1)S(1)}, bf16[128,32,256]{2,1,0:T(8,128)(2,1)}, u32[]{:S(2)}) copy-start(bf16[128,32,256]{2,1,0:T(8,128)(2,1)} %copy-done) | copy-start | bytes 6291460
  92.2 2.2 %copy-start.2 = (f32[1,1024,1024]{2,1,0:T(8,128)S(1)}, f32[1,1024,1024]{2,1,0:T(8,128)}, u32[]{:S(2)}) copy-start(f32[1,1024,1024]{2,1,0:T(8,128)} %left.2) | copy-start | bytes 12582916
  94.3 2.2 %copy-start.3 = (f32[1,1024,1024]{2,1,0:T(8,128)S(1)}, f32[1,1024,1024]{2,1,0:T(8,128)}, u32[]{:S(2)}) copy-start(f32[1,1024,1024]{2,1,0:T(8,128)} %right.2) | copy-start | bytes 12582916

commit v3 on v2

--- a/solution.py
+++ b/solution.py
@@ -10,6 +10,7 @@
 DECAY = 0.95
 EPSILON = 1e-06
 MIB = 1 << 20
+STAGE_GROUPS = (2, 2, 2)
 
 
 def params(mib):
@@ -24,18 +25,19 @@
     return (reps - 1 - me, me ^ 1)[part % 2]
 
 
-def pack_kernel(grads, *rest, parts, own, groups, columns, reps, width):
+def pack_kernel(grads, *rest, parts, spans, own, columns, reps, width):
     outs, sem = rest[:-1], rest[-1]
     me = lax.axis_index("rep")
     copies = []
     for out, part in zip(outs, parts):
+        start, groups = spans[part]
         target = me if own else first_partner(part, me, reps)
         for which, strip in enumerate((target, second_partner(part, target, reps))):
             for column in range(columns):
                 offset = pl.multiple_of((column * reps + strip) * width, width)
                 copies.append(
                     pltpu.make_async_copy(
-                        grads.at[0, pl.ds(part * groups, groups), :, pl.ds(offset, width)],
+                        grads.at[0, pl.ds(start, groups), :, pl.ds(offset, width)],
                         out.at[which, column],
                         sem.at[len(copies)],
                     )
@@ -46,13 +48,14 @@
         copy.wait()
 
 
-def pack(grads, parts, own, groups, columns, reps, width):
-    shape = jax.ShapeDtypeStruct((2, columns, groups, grads.shape[2], width), grads.dtype)
+def pack(grads, parts, spans, own, columns, reps, width):
     return pl.pallas_call(
         functools.partial(
-            pack_kernel, parts=parts, own=own, groups=groups, columns=columns, reps=reps, width=width
+            pack_kernel, parts=parts, spans=spans, own=own, columns=columns, reps=reps, width=width
         ),
-        out_shape=[shape] * len(parts),
+        out_shape=[
+            jax.ShapeDtypeStruct((2, columns, spans[part][1], grads.shape[2], width), grads.dtype) for part in parts
+        ],
         in_specs=[pl.BlockSpec(memory_space=pltpu.HBM)],
         out_specs=[pl.BlockSpec(memory_space=pl.ANY)] * len(parts),
         scratch_shapes=[pltpu.SemaphoreType.DMA((2 * columns * len(parts),))],
@@ -80,22 +83,23 @@
     )(own, received)
 
 
-def second_sum_kernel(owners, *refs, parts, columns, groups, initial):
+def second_sum_kernel(owners, *refs, parts, spans, columns, initial):
     out = refs[-1]
     if initial:
         out[...] = jnp.zeros_like(out)
     for index, part in enumerate(parts):
         own, first, second = refs[3 * index : 3 * index + 3]
+        start, groups = spans[part]
         for group in range(groups):
             for column in range(columns):
-                owner = owners[(part * groups + group) * columns + column]
+                owner = owners[(start + group) * columns + column]
                 total = own[0, column, group].astype(jnp.float32) + first[0, column, group].astype(jnp.float32)
                 total += second[column, group].astype(jnp.float32)
                 out[owner] = total.astype(out.dtype)
 
 
-def second_sum(owners, terms, parts, devices, before=None):
-    _, columns, groups, height, width = terms[0][0].shape
+def second_sum(owners, terms, parts, spans, devices, before=None):
+    _, columns, _, height, width = terms[0][0].shape
     arrays = [array for part in parts for array in terms[part]]
     aliases = {}
     if before is not None:
@@ -103,7 +107,7 @@
         aliases = {len(arrays): 0}
     return pl.pallas_call(
         functools.partial(
-            second_sum_kernel, parts=parts, columns=columns, groups=groups, initial=before is None
+            second_sum_kernel, parts=parts, spans=spans, columns=columns, initial=before is None
         ),
         out_shape=jax.ShapeDtypeStruct((devices, height, width), arrays[0].dtype),
         in_specs=[pl.BlockSpec(memory_space=pltpu.SMEM)] + [pl.BlockSpec(memory_space=pltpu.VMEM)] * len(arrays),
@@ -200,33 +204,30 @@
     )(grad, left, right)
 
 
-def pick_kernel(owners, returned, out, sem, *, columns, size):
-    groups = out.shape[0]
+def pick_kernel(owners, returned, out, gathered, sem, *, columns, size, steps):
+    groups = out.shape[0] // steps
     copies = []
-    for group in range(groups):
-        for column in range(columns):
-            block = group * columns + column
-            copies.append(
-                pltpu.make_async_copy(
-                    returned.at[owners[block]],
-                    out.at[group, :, pl.ds(column * size, size)],
-                    sem.at[block],
-                )
-            )
-    for copy in copies:
-        copy.start()
+    for step in range(steps):
+        band = pl.ds(step * groups, groups)
+        for group in range(step * groups, (step + 1) * groups):
+            for column in range(columns):
+                piece = returned[owners[group * columns + column]]
+                gathered[group, :, column * size : (column + 1) * size] = piece
+        copies.append(pltpu.make_async_copy(gathered.at[band], out.at[band], sem.at[step]))
+        copies[-1].start()
     for copy in copies:
         copy.wait()
 
 
-def pick(owners, returned, groups, columns):
+def pick(owners, returned, groups, columns, steps=6):
     _, rows, size = returned.shape
-    return pl.pallas_call(
-        functools.partial(pick_kernel, columns=columns, size=size),
-        out_shape=jax.ShapeDtypeStruct((groups, rows, columns * size), returned.dtype),
-        in_specs=[pl.BlockSpec(memory_space=pltpu.SMEM), pl.BlockSpec(memory_space=pl.ANY)],
-        out_specs=pl.BlockSpec(memory_space=pl.ANY),
-        scratch_shapes=[pltpu.SemaphoreType.DMA((groups * columns,))],
+    shape = (groups, rows, columns * size)
+    return pl.pallas_call(
+        functools.partial(pick_kernel, columns=columns, size=size, steps=steps),
+        out_shape=pltpu.HBM(shape, returned.dtype),
+        in_specs=[pl.BlockSpec(memory_space=pltpu.SMEM), pl.BlockSpec(memory_space=pltpu.VMEM)],
+        out_specs=pl.BlockSpec(memory_space=pltpu.HBM),
+        scratch_shapes=[pltpu.VMEM(shape, returned.dtype), pltpu.SemaphoreType.DMA((steps,))],
         compiler_params=params(16),
         name="pick",
     )(owners, returned)
@@ -246,18 +247,25 @@
     matches = owner_block[None, :] == lax.iota(jnp.int32, groups * columns)[:, None]
     owners = jnp.sum(jnp.where(matches, lax.iota(jnp.int32, devices)[None, :], 0), axis=1)
 
-    parts = 4
-    part_groups = groups // parts
-    sizes = (part_groups, columns, reps, width)
-    packed = pack(grads, (0, 1), False, *sizes) + pack(grads, (2, 3), False, *sizes)
-    firsts = [lax.ppermute(packed[part], "rep", orders[part % 2][0]) for part in range(parts)]
-    own = pack(grads, tuple(range(parts)), True, *sizes)
+    stages = len(STAGE_GROUPS)
+    spans, start = [], 0
+    for count in STAGE_GROUPS:
+        for _ in range(2):
+            spans.append((start, count))
+            start += count
+    parts = range(2 * stages)
+    pairs = [(2 * stage, 2 * stage + 1) for stage in range(stages)]
+    sizes = (columns, reps, width)
+    packed = [part for pair in pairs for part in pack(grads, pair, spans, False, *sizes)]
+    firsts = [lax.ppermute(packed[part], "rep", orders[part % 2][0]) for part in parts]
+    own = pack(grads, tuple(parts), spans, True, *sizes)
     seconds = [
-        lax.ppermute(first_sum(own[part], firsts[part]), "rep", orders[part % 2][1]) for part in range(parts)
+        lax.ppermute(first_sum(own[part], firsts[part]), "rep", orders[part % 2][1]) for part in parts
     ]
     terms = list(zip(own, firsts, seconds))
-    pieces = second_sum(owners, terms, (0, 1), devices)
-    pieces = second_sum(owners, terms, (2, 3), devices, pieces)
+    pieces = None
+    for pair in pairs:
+        pieces = second_sum(owners, terms, pair, spans, devices, pieces)
     grad_block = lax.all_to_all(pieces, ("rep", "fsdp"), split_axis=0, concat_axis=0, tiled=True)
     grad_block = grad_block.reshape(reps, size, width)
     update_block = block_update(root_left, grad_block, root_right)

time: 124 us -> 123 us (level)
  waiting for transfers between devices: 40.7 us -> 33.4 us
  starting transfers between devices: 13.7 us -> 19.1 us
    ppermute x4 -> x6, waiting for transfers between devices: 15.2 us -> 8.81 us  [body(): lax.ppermute(packed[part], 'rep', orders[part % 2][0])]
    ppermute x4 -> x6, starting transfers between devices: 3.74 us -> 7.08 us  [body(): lax.ppermute(first_sum(own[part], firsts[part]), 'rep', orders[part % 2][1])]
    ppermute x4 -> x6, starting transfers between devices: 5.28 us -> 7.34 us  [body(): lax.ppermute(packed[part], 'rep', orders[part % 2][0])]
    pallas_call x6 -> x8, Pallas kernels: 8.2 us -> 9.33 us  [the longest x4 5.69 us: pack(): pl.pallas_call(functools.partial(pack_kernel, parts=parts, spans=spans, o...]
    ppermute x4 -> x6, waiting for transfers between devices: 7.74 us -> 6.88 us  [body(): lax.ppermute(first_sum(own[part], firsts[part]), 'rep', orders[part % 2][1])]
  transfers between devices with their start and end apart: 9 -> 13, of which waited for: 7 -> 7; matrix products, arithmetic and copies ran while one was open for 0% -> 0% of each run, Pallas kernels for 9% -> 10%
where the time goes in v3:
time: 123 us; the launch traced here: 122 us
  blocking collectives  40.2 us (33%)
  waiting for transfers between devices  33.4 us (27%)
  Pallas kernels  22.6 us (18%)
  starting transfers between devices  19.1 us (16%)
  local copies, waits for them, and re-layouts  5.98 us (5%)
    all_to_all x1, blocking collectives, body(): lax.all_to_all(pieces, ('rep', 'fsdp'), split_axis=0, concat_axis=0, tile...  40.2 us
    all_to_all x1, waiting for transfers between devices, body(): lax.all_to_all(update_block.reshape(devices, size // devices, size), ('re...  17.7 us
    ppermute x6, waiting for transfers between devices, body(): lax.ppermute(packed[part], 'rep', orders[part % 2][0])  8.81 us
    ppermute x6, starting transfers between devices, body(): lax.ppermute(packed[part], 'rep', orders[part % 2][0])  7.34 us
    ppermute x6, starting transfers between devices, body(): lax.ppermute(first_sum(own[part], firsts[part]), 'rep', orders[part % 2][1])  7.08 us
    ppermute x6, waiting for transfers between devices, body(): lax.ppermute(first_sum(own[part], firsts[part]), 'rep', orders[part % 2][1])  6.88 us
    pallas_call x1, Pallas kernels, statistics(): pl.pallas_call(statistics_kernel, grid=(strips,), out_shape=[jax.ShapeDty...  6.7 us
    pallas_call x1, Pallas kernels, block_update(): pl.pallas_call(functools.partial(update_kernel, tiles=tiles, out_tiles=ou...  6.34 us
  transfers between devices with their start and end apart: 13, of which 7 were waited for; matrix products, arithmetic and copies ran while one was open for 0% of the time, Pallas kernels for 10%

profile of v3, /device:TPU:1, one launch (start us, length us, event | category | flops | bytes accessed | tf_op | source)
XLA Modules:
  0.0 122.3 jit_solution(9848772460242575981)
XLA Ops:
  0.6 1.2 %pack.5 = (bf16[2,5,2,32,256]{4,3,2,1,0:T(8,128)(2,1)S(1)}, bf16[2,5,2,32,256]{4,3,2,1,0:T(8,128)(2,1)S(1)}) custom-call(bf16[1,12,32,5120]{3,2,1,0:T(8,128)(2,1)} %grads.7), custom_call_target="tpu_custom_call" | custom-call | tf_op jit(solution)/shard_map/pack/pallas_call | solution.py:52
  1.9 3.6 %collective-permute-start.10 = (bf16[2,5,2,32,256]{4,3,2,1,0:T(8,128)(2,1)S(1)}, bf16[2,5,2,32,256]{4,3,2,1,0:T(8,128)(2,1)S(1)}, u32[]{:S(2)}, u32[]{:S(2)}) collective-permute-start(bf16[2,5,2,32,256]{4,3,2,1,0:T(8,128)(2,1)S(1)} %get-tuple-element.28), channel_id=1, source_target_pairs={{0,96},{32,64},{64,32},{96,0},{1,97},{33,65},{65,33},{97,1},{2,98}... | collective-permute-start | bytes 983048 | tf_op jit(solution)/shard_map/ppermute | solution.py:260
  5.5 0.0 collective-permute-start.8
  5.5 1.2 %pack.4 = (bf16[2,5,2,32,256]{4,3,2,1,0:T(8,128)(2,1)S(1)}, bf16[2,5,2,32,256]{4,3,2,1,0:T(8,128)(2,1)S(1)}) custom-call(bf16[1,12,32,5120]{3,2,1,0:T(8,128)(2,1)} %grads.7), custom_call_target="tpu_custom_call" | custom-call | tf_op jit(solution)/shard_map/pack/pallas_call | solution.py:52
  6.8 0.7 collective-permute-start.6
  7.5 0.9 collective-permute-start.4
  8.4 1.2 pack.3
  9.6 2.1 %collective-permute-start.2 = (bf16[2,5,2,32,256]{4,3,2,1,0:T(8,128)(2,1)S(1)}, bf16[2,5,2,32,256]{4,3,2,1,0:T(8,128)(2,1)S(1)}, u32[]{:S(2)}, u32[]{:S(2)}) collective-permute-start(bf16[2,5,2,32,256]{4,3,2,1,0:T(8,128)(2,1)S(1)} %get-tuple-element.20), channel_id=1, source_target_pairs={{0,96},{32,64},{64,32},{96,0},{1,97},{33,65},{65,33},{97,1},{2,98}... | collective-permute-start | bytes 983048 | tf_op jit(solution)/shard_map/ppermute | solution.py:260
  11.7 1.1 collective-permute-done.10.received.refs_4_
  12.8 0.0 collective-permute-start
  12.8 2.0 %pack_own.1 = (bf16[2,5,2,32,256]{4,3,2,1,0:T(8,128)(2,1)S(1)}, bf16[2,5,2,32,256]{4,3,2,1,0:T(8,128)(2,1)S(1)}, bf16[2,5,2,32,256]{4,3,2,1,0:T(8,128)(2,1)S(1)}...) custom-call(bf16[1,12,32,5120]{3,2,1,0:T(8,128)(2,1)} %grads.7), custom_call_target="tpu_custom_call" | custom-call | tf_op jit(solution)/shard_map/pack_own/pallas_call | solution.py:52
  14.9 0.0 copy-start.6
  14.9 0.0 collective-permute-done.8.received.refs_1_
  14.9 1.5 %collective-permute-start.11 = (bf16[5,2,32,256]{3,2,1,0:T(8,128)(2,1)S(1)}, bf16[5,2,32,256]{3,2,1,0:T(8,128)(2,1)S(1)}, u32[]{:S(2)}, u32[]{:S(2)}) collective-permute-start(bf16[5,2,32,256]{3,2,1,0:T(8,128)(2,1)S(1)} %first_sum.11), channel_id=1, source_target_pairs={{0,32},{32,0},{64,96},{96,64},{1,33},{33,1},{65,97},{97,65},{2,34}... | collective-permute-start | bytes 491528 | tf_op jit(solution)/shard_map/ppermute | solution.py:263
  16.5 3.4 %collective-permute-done.6.received.refs_4_ = bf16[2,5,2,32,256]{4,3,2,1,0:T(8,128)(2,1)S(1)} collective-permute-done((bf16[2,5,2,32,256]{4,3,2,1,0:T(8,128)(2,1)S(1)}, bf16[2,5,2,32,256]{4,3,2,1,0:T(8,128)(2,1)S(1)}, u32[]{:S(2)}, u32[]{:S(2)}) %collective-permute-start.6) | collective-permute-done | bytes 327712 | tf_op jit(solution)/shard_map/ppermute | solution.py:260
  19.8 2.5 %collective-permute-start.9 = (bf16[5,2,32,256]{3,2,1,0:T(8,128)(2,1)S(1)}, bf16[5,2,32,256]{3,2,1,0:T(8,128)(2,1)S(1)}, u32[]{:S(2)}, u32[]{:S(2)}) collective-permute-start(bf16[5,2,32,256]{3,2,1,0:T(8,128)(2,1)S(1)} %first_sum.10), channel_id=1, source_target_pairs={{0,96},{32,64},{64,32},{96,0},{1,97},{33,65},{65,33},{97,1},{2,98}... | collective-permute-start | bytes 491528 | tf_op jit(solution)/shard_map/ppermute | solution.py:263
  22.4 0.0 collective-permute-done.4.received.refs_1_
  22.4 0.1 collective-permute-start.7
  22.5 4.3 %collective-permute-done.2.received.refs_4_ = bf16[2,5,2,32,256]{4,3,2,1,0:T(8,128)(2,1)S(1)} collective-permute-done((bf16[2,5,2,32,256]{4,3,2,1,0:T(8,128)(2,1)S(1)}, bf16[2,5,2,32,256]{4,3,2,1,0:T(8,128)(2,1)S(1)}, u32[]{:S(2)}, u32[]{:S(2)}) %collective-permute-start.2) | collective-permute-done | bytes 327712 | tf_op jit(solution)/shard_map/ppermute | solution.py:260
  26.9 2.5 %collective-permute-start.5 = (bf16[5,2,32,256]{3,2,1,0:T(8,128)(2,1)S(1)}, bf16[5,2,32,256]{3,2,1,0:T(8,128)(2,1)S(1)}, u32[]{:S(2)}, u32[]{:S(2)}) collective-permute-start(bf16[5,2,32,256]{3,2,1,0:T(8,128)(2,1)S(1)} %first_sum.8), channel_id=1, source_target_pairs={{0,96},{32,64},{64,32},{96,0},{1,97},{33,65},{65,33},{97,1},{2,98}... | collective-permute-start | bytes 491528 | tf_op jit(solution)/shard_map/ppermute | solution.py:263
  29.4 0.0 collective-permute-done.received.refs_1_
  29.4 0.1 collective-permute-start.3
  29.6 1.8 %collective-permute-done.11.refs_5_ = bf16[5,2,32,256]{3,2,1,0:T(8,128)(2,1)S(1)} collective-permute-done((bf16[5,2,32,256]{3,2,1,0:T(8,128)(2,1)S(1)}, bf16[5,2,32,256]{3,2,1,0:T(8,128)(2,1)S(1)}, u32[]{:S(2)}, u32[]{:S(2)}) %collective-permute-start.11) | collective-permute-done | bytes 163872 | tf_op jit(solution)/shard_map/ppermute | solution.py:263
  31.3 0.4 collective-permute-start.1
  31.7 0.0 copy-done.6
  31.7 0.1 select_reduce_fusion.owners
  31.8 0.0 collective-permute-done.9.refs_2_
  31.8 0.8 second_sum.3.refs_6_
  32.6 2.2 %collective-permute-done.7.refs_5_ = bf16[5,2,32,256]{3,2,1,0:T(8,128)(2,1)S(1)} collective-permute-done((bf16[5,2,32,256]{3,2,1,0:T(8,128)(2,1)S(1)}, bf16[5,2,32,256]{3,2,1,0:T(8,128)(2,1)S(1)}, u32[]{:S(2)}, u32[]{:S(2)}) %collective-permute-start.7) | collective-permute-done | bytes 163872 | tf_op jit(solution)/shard_map/ppermute | solution.py:263
  34.9 0.0 collective-permute-done.5.refs_2_
  34.9 0.7 second_sum.4.refs_6_
  35.5 2.8 %collective-permute-done.3.refs_5_ = bf16[5,2,32,256]{3,2,1,0:T(8,128)(2,1)S(1)} collective-permute-done((bf16[5,2,32,256]{3,2,1,0:T(8,128)(2,1)S(1)}, bf16[5,2,32,256]{3,2,1,0:T(8,128)(2,1)S(1)}, u32[]{:S(2)}, u32[]{:S(2)}) %collective-permute-start.3) | collective-permute-done | bytes 163872 | tf_op jit(solution)/shard_map/ppermute | solution.py:263
  38.4 0.0 collective-permute-done.1.refs_2_
  38.4 0.7 second_sum.5
  39.0 0.0 copy-start.4
  39.0 0.0 copy-start.5
  39.1 40.2 %all_to_all.10 = bf16[128,32,256]{2,1,0:T(8,128)(2,1)S(1)} all-to-all(bf16[128,32,256]{2,1,0:T(8,128)(2,1)S(1)} %second_sum.5), channel_id=1, replica_groups=mesh['rep'=4,'fsdp'=32] {'rep','fsdp'}, dimensions={0} | all-to-all | bytes 4194304 | tf_op jit(solution)/shard_map/all_to_all | solution.py:269
  79.3 0.0 copy-start
  79.3 0.0 copy-done.4
  79.3 0.0 copy-done.5
  79.3 6.3 %block_update.1 = bf16[1024,1024]{1,0:T(8,128)(2,1)} custom-call(bf16[1,1024,1024]{2,1,0:T(8,128)(2,1)S(1)} %copy-done.4, bf16[4,1024,256]{2,1,0:T(8,128)(2,1)S(1)} %bitcast.2, bf16[1,1024,1024]{2,1,0:T(8,128)(2,1)S(1)} %copy-done.5), custom_call_target="tpu_custom_call" | custom-call | flops 4294967296 | bytes 8388608 | tf_op jit(solution)/shard_map/block_update/pallas_call | solution.py:158
  85.7 0.0 copy-done
  85.7 4.7 %all-to-all-start.1 = ((bf16[128,8,1024]{2,1,0:T(8,128)(2,1)}), bf16[128,8,1024]{2,1,0:T(8,128)(2,1)S(1)}, u32[]{:S(2)}, u32[]{:S(2)}) async-start(bf16[128,8,1024]{2,1,0:T(8,128)(2,1)} %bitcast.4), calls=%async_computation.1 | async-start | bytes 4194304 | tf_op jit(solution)/shard_map/all_to_all | solution.py:272
  90.4 0.0 copy-start.1
  90.4 1.6 %copy-done.1 = bf16[128,32,256]{2,1,0:T(8,128)(2,1)S(1)} copy-done((bf16[128,32,256]{2,1,0:T(8,128)(2,1)S(1)}, bf16[128,32,256]{2,1,0:T(8,128)(2,1)}, u32[]{:S(2)}) %copy-start.1) | copy-done | bytes 2097176
  92.0 0.0 copy-start.2
  92.0 2.2 %copy-done.2 = f32[1,1024,1024]{2,1,0:T(8,128)S(1)} copy-done((f32[1,1024,1024]{2,1,0:T(8,128)S(1)}, f32[1,1024,1024]{2,1,0:T(8,128)}, u32[]{:S(2)}) %copy-start.2) | copy-done | bytes 4194328
  94.2 0.0 copy-start.3
  94.2 2.2 %copy-done.3 = f32[1,1024,1024]{2,1,0:T(8,128)S(1)} copy-done((f32[1,1024,1024]{2,1,0:T(8,128)S(1)}, f32[1,1024,1024]{2,1,0:T(8,128)}, u32[]{:S(2)}) %copy-start.3) | copy-done | bytes 4194328
  96.4 6.7 %statistics.1 = (f32[1,1024,1024]{2,1,0:T(8,128)}, f32[1,1024,1024]{2,1,0:T(8,128)}) custom-call(bf16[4,1024,256]{2,1,0:T(8,128)(2,1)S(1)} %bitcast.3, f32[1,1024,1024]{2,1,0:T(8,128)S(1)} %copy-done.2, f32[1,1024,1024]{2,1,0:T(8,128)S(1)} %copy-done.3), custom_call_target="tpu_custom_call" | custom-call | flops 4294967296 | bytes 18874368 | tf_op jit(solution)/shard_map/statistics/pallas_call | solution.py:195
  103.1 17.7 %all-to-all-done.1.returned = bf16[128,8,1024]{2,1,0:T(8,128)(2,1)S(1)} async-done(((bf16[128,8,1024]{2,1,0:T(8,128)(2,1)}), bf16[128,8,1024]{2,1,0:T(8,128)(2,1)S(1)}, u32[]{:S(2)}, u32[]{:S(2)}) %all-to-all-start.1) | async-done | bytes 2097184 | tf_op jit(solution)/shard_map/all_to_all | solution.py:272
  120.8 1.5 %pick.1 = bf16[12,8,5120]{2,1,0:T(8,128)(2,1)} custom-call(s32[60]{0:T(128)S(1)} %select_reduce_fusion.owners, bf16[128,8,1024]{2,1,0:T(8,128)(2,1)S(1)} %all-to-all-done.1.returned), custom_call_target="tpu_custom_call" | custom-call | tf_op jit(solution)/shard_map/pick/pallas_call | solution.py:225
  (6 shorter events, 0.2 us)
Async XLA Ops:
  1.9 10.9 %collective-permute-start.10 = (bf16[2,5,2,32,256]{4,3,2,1,0:T(8,128)(2,1)S(1)}, bf16[2,5,2,32,256]{4,3,2,1,0:T(8,128)(2,1)S(1)}, u32[]{:S(2)}, u32[]{:S(2)}) collective-permute-start(bf16[2,5,2,32,256]{4,3,2,1,0:T(8,128)(2,1)S(1)} %get-tuple-element.28), channel_id=1, source_target_pairs={{0,96},{32,64},{64,32},{96,0},{1,97},{33,65},{65,33},{97,1},{2,98}... | collective-permute-start | bytes 983048 | tf_op jit(solution)/shard_map/ppermute | solution.py:260
  5.5 9.4 %collective-permute-start.8 = (bf16[2,5,2,32,256]{4,3,2,1,0:T(8,128)(2,1)S(1)}, bf16[2,5,2,32,256]{4,3,2,1,0:T(8,128)(2,1)S(1)}, u32[]{:S(2)}, u32[]{:S(2)}) collective-permute-start(bf16[2,5,2,32,256]{4,3,2,1,0:T(8,128)(2,1)S(1)} %get-tuple-element.26), channel_id=1, source_target_pairs={{0,32},{32,0},{64,96},{96,64},{1,33},{33,1},{65,97},{97,65},{2,34}... | collective-permute-start | bytes 983048 | tf_op jit(solution)/shard_map/ppermute | solution.py:260
  6.8 13.1 %collective-permute-start.6 = (bf16[2,5,2,32,256]{4,3,2,1,0:T(8,128)(2,1)S(1)}, bf16[2,5,2,32,256]{4,3,2,1,0:T(8,128)(2,1)S(1)}, u32[]{:S(2)}, u32[]{:S(2)}) collective-permute-start(bf16[2,5,2,32,256]{4,3,2,1,0:T(8,128)(2,1)S(1)} %get-tuple-element.24), channel_id=1, source_target_pairs={{0,96},{32,64},{64,32},{96,0},{1,97},{33,65},{65,33},{97,1},{2,98}... | collective-permute-start | bytes 983048 | tf_op jit(solution)/shard_map/ppermute | solution.py:260
  7.5 14.9 %collective-permute-start.4 = (bf16[2,5,2,32,256]{4,3,2,1,0:T(8,128)(2,1)S(1)}, bf16[2,5,2,32,256]{4,3,2,1,0:T(8,128)(2,1)S(1)}, u32[]{:S(2)}, u32[]{:S(2)}) collective-permute-start(bf16[2,5,2,32,256]{4,3,2,1,0:T(8,128)(2,1)S(1)} %get-tuple-element.22), channel_id=1, source_target_pairs={{0,32},{32,0},{64,96},{96,64},{1,33},{33,1},{65,97},{97,65},{2,34}... | collective-permute-start | bytes 983048 | tf_op jit(solution)/shard_map/ppermute | solution.py:260
  9.6 17.2 %collective-permute-start.2 = (bf16[2,5,2,32,256]{4,3,2,1,0:T(8,128)(2,1)S(1)}, bf16[2,5,2,32,256]{4,3,2,1,0:T(8,128)(2,1)S(1)}, u32[]{:S(2)}, u32[]{:S(2)}) collective-permute-start(bf16[2,5,2,32,256]{4,3,2,1,0:T(8,128)(2,1)S(1)} %get-tuple-element.20), channel_id=1, source_target_pairs={{0,96},{32,64},{64,32},{96,0},{1,97},{33,65},{65,33},{97,1},{2,98}... | collective-permute-start | bytes 983048 | tf_op jit(solution)/shard_map/ppermute | solution.py:260
  12.8 16.6 %collective-permute-start = (bf16[2,5,2,32,256]{4,3,2,1,0:T(8,128)(2,1)S(1)}, bf16[2,5,2,32,256]{4,3,2,1,0:T(8,128)(2,1)S(1)}, u32[]{:S(2)}, u32[]{:S(2)}) collective-permute-start(bf16[2,5,2,32,256]{4,3,2,1,0:T(8,128)(2,1)S(1)} %get-tuple-element.18), channel_id=1, source_target_pairs={{0,32},{32,0},{64,96},{96,64},{1,33},{33,1},{65,97},{97,65},{2,34}... | collective-permute-start | bytes 983048 | tf_op jit(solution)/shard_map/ppermute | solution.py:260
  14.9 16.8 %copy-start.6 = (s32[128]{0:T(128)S(1)}, s32[128]{0:T(128)}, u32[]{:S(2)}) copy-start(s32[128]{0:T(128)} %param.11) | copy-start | bytes 1540
  14.9 16.5 %collective-permute-start.11 = (bf16[5,2,32,256]{3,2,1,0:T(8,128)(2,1)S(1)}, bf16[5,2,32,256]{3,2,1,0:T(8,128)(2,1)S(1)}, u32[]{:S(2)}, u32[]{:S(2)}) collective-permute-start(bf16[5,2,32,256]{3,2,1,0:T(8,128)(2,1)S(1)} %first_sum.11), channel_id=1, source_target_pairs={{0,32},{32,0},{64,96},{96,64},{1,33},{33,1},{65,97},{97,65},{2,34}... | collective-permute-start | bytes 491528 | tf_op jit(solution)/shard_map/ppermute | solution.py:263
  19.8 12.0 %collective-permute-start.9 = (bf16[5,2,32,256]{3,2,1,0:T(8,128)(2,1)S(1)}, bf16[5,2,32,256]{3,2,1,0:T(8,128)(2,1)S(1)}, u32[]{:S(2)}, u32[]{:S(2)}) collective-permute-start(bf16[5,2,32,256]{3,2,1,0:T(8,128)(2,1)S(1)} %first_sum.10), channel_id=1, source_target_pairs={{0,96},{32,64},{64,32},{96,0},{1,97},{33,65},{65,33},{97,1},{2,98}... | collective-permute-start | bytes 491528 | tf_op jit(solution)/shard_map/ppermute | solution.py:263
  22.4 12.5 %collective-permute-start.7 = (bf16[5,2,32,256]{3,2,1,0:T(8,128)(2,1)S(1)}, bf16[5,2,32,256]{3,2,1,0:T(8,128)(2,1)S(1)}, u32[]{:S(2)}, u32[]{:S(2)}) collective-permute-start(bf16[5,2,32,256]{3,2,1,0:T(8,128)(2,1)S(1)} %first_sum.9), channel_id=1, source_target_pairs={{0,32},{32,0},{64,96},{96,64},{1,33},{33,1},{65,97},{97,65},{2,34}... | collective-permute-start | bytes 491528 | tf_op jit(solution)/shard_map/ppermute | solution.py:263
  26.9 8.0 %collective-permute-start.5 = (bf16[5,2,32,256]{3,2,1,0:T(8,128)(2,1)S(1)}, bf16[5,2,32,256]{3,2,1,0:T(8,128)(2,1)S(1)}, u32[]{:S(2)}, u32[]{:S(2)}) collective-permute-start(bf16[5,2,32,256]{3,2,1,0:T(8,128)(2,1)S(1)} %first_sum.8), channel_id=1, source_target_pairs={{0,96},{32,64},{64,32},{96,0},{1,97},{33,65},{65,33},{97,1},{2,98}... | collective-permute-start | bytes 491528 | tf_op jit(solution)/shard_map/ppermute | solution.py:263
  29.4 9.0 %collective-permute-start.3 = (bf16[5,2,32,256]{3,2,1,0:T(8,128)(2,1)S(1)}, bf16[5,2,32,256]{3,2,1,0:T(8,128)(2,1)S(1)}, u32[]{:S(2)}, u32[]{:S(2)}) collective-permute-start(bf16[5,2,32,256]{3,2,1,0:T(8,128)(2,1)S(1)} %first_sum.7), channel_id=1, source_target_pairs={{0,32},{32,0},{64,96},{96,64},{1,33},{33,1},{65,97},{97,65},{2,34}... | collective-permute-start | bytes 491528 | tf_op jit(solution)/shard_map/ppermute | solution.py:263
  31.3 7.0 %collective-permute-start.1 = (bf16[5,2,32,256]{3,2,1,0:T(8,128)(2,1)S(1)}, bf16[5,2,32,256]{3,2,1,0:T(8,128)(2,1)S(1)}, u32[]{:S(2)}, u32[]{:S(2)}) collective-permute-start(bf16[5,2,32,256]{3,2,1,0:T(8,128)(2,1)S(1)} %first_sum.6), channel_id=1, source_target_pairs={{0,96},{32,64},{64,32},{96,0},{1,97},{33,65},{65,33},{97,1},{2,98}... | collective-permute-start | bytes 491528 | tf_op jit(solution)/shard_map/ppermute | solution.py:263
  39.0 40.3 %copy-start.4 = (bf16[1,1024,1024]{2,1,0:T(8,128)(2,1)S(1)}, bf16[1,1024,1024]{2,1,0:T(8,128)(2,1)}, u32[]{:S(2)}) copy-start(bf16[1,1024,1024]{2,1,0:T(8,128)(2,1)} %left.3) | copy-start | bytes 6291460
  39.0 40.3 %copy-start.5 = (bf16[1,1024,1024]{2,1,0:T(8,128)(2,1)S(1)}, bf16[1,1024,1024]{2,1,0:T(8,128)(2,1)}, u32[]{:S(2)}) copy-start(bf16[1,1024,1024]{2,1,0:T(8,128)(2,1)} %right.3) | copy-start | bytes 6291460
  79.3 6.4 %copy-start = (bf16[128,32,256]{2,1,0:T(8,128)(2,1)}, bf16[128,32,256]{2,1,0:T(8,128)(2,1)S(1)}, u32[]{:S(2)}) copy-start(bf16[128,32,256]{2,1,0:T(8,128)(2,1)S(1)} %all_to_all.10) | copy-start | bytes 6291460
  85.7 35.1 %all-to-all-start.1 = ((bf16[128,8,1024]{2,1,0:T(8,128)(2,1)}), bf16[128,8,1024]{2,1,0:T(8,128)(2,1)S(1)}, u32[]{:S(2)}, u32[]{:S(2)}) async-start(bf16[128,8,1024]{2,1,0:T(8,128)(2,1)} %bitcast.4), calls=%async_computation.1 | async-start | bytes 4194304 | tf_op jit(solution)/shard_map/all_to_all | solution.py:272
  90.4 1.6 %copy-start.1 = (bf16[128,32,256]{2,1,0:T(8,128)(2,1)S(1)}, bf16[128,32,256]{2,1,0:T(8,128)(2,1)}, u32[]{:S(2)}) copy-start(bf16[128,32,256]{2,1,0:T(8,128)(2,1)} %copy-done) | copy-start | bytes 6291460
  92.0 2.2 %copy-start.2 = (f32[1,1024,1024]{2,1,0:T(8,128)S(1)}, f32[1,1024,1024]{2,1,0:T(8,128)}, u32[]{:S(2)}) copy-start(f32[1,1024,1024]{2,1,0:T(8,128)} %left.2) | copy-start | bytes 12582916
  94.2 2.2 %copy-start.3 = (f32[1,1024,1024]{2,1,0:T(8,128)S(1)}, f32[1,1024,1024]{2,1,0:T(8,128)}, u32[]{:S(2)}) copy-start(f32[1,1024,1024]{2,1,0:T(8,128)} %right.2) | copy-start | bytes 12582916

commit v4 on v3

--- a/solution.py
+++ b/solution.py
@@ -142,10 +142,11 @@
     mean_grad = jnp.full((8, 128), jnp.sum(grad_square) / entries)
     mean_precond = jnp.full((8, 128), jnp.sum(square) / entries)
     scale = jnp.sqrt(mean_grad / (mean_precond + EPSILON))[0:1, 0:1]
-    out_rows = size // out_tiles
+    eighth = size // (2 * out_tiles)
+    edges = [0] + list(range(eighth, size, 2 * eighth)) + [size]
     copies = []
-    for tile in range(out_tiles):
-        band = slice(tile * out_rows, (tile + 1) * out_rows)
+    for tile, (start, end) in enumerate(zip(edges[:-1], edges[1:])):
+        band = slice(start, end)
         scaled[band, :] = (precond[band, :] * scale).astype(out.dtype)
         copies.append(pltpu.make_async_copy(scaled.at[band, :], out.at[band, :], sem.at[tile]))
         copies[-1].start()
@@ -163,7 +164,7 @@
         scratch_shapes=[
             pltpu.VMEM((size, size), jnp.float32),
             pltpu.VMEM((size, size), jnp.bfloat16),
-            pltpu.SemaphoreType.DMA((out_tiles,)),
+            pltpu.SemaphoreType.DMA((out_tiles + 1,)),
         ],
         compiler_params=params(32),
         cost_estimate=pl.CostEstimate(flops=4 * size**3, bytes_accessed=8 * size * size, transcendentals=0),
@@ -257,8 +258,9 @@
     pairs = [(2 * stage, 2 * stage + 1) for stage in range(stages)]
     sizes = (columns, reps, width)
     packed = [part for pair in pairs for part in pack(grads, pair, spans, False, *sizes)]
+    own = pack(grads, tuple(parts), spans, True, *sizes)
+    packed[-2:], own = lax.optimization_barrier((packed[-2:], own))
     firsts = [lax.ppermute(packed[part], "rep", orders[part % 2][0]) for part in parts]
-    own = pack(grads, tuple(parts), spans, True, *sizes)
     seconds = [
         lax.ppermute(first_sum(own[part], firsts[part]), "rep", orders[part % 2][1]) for part in parts
     ]

time: 123 us -> 123 us (level)
    ppermute x6, waiting for transfers between devices: 8.81 us -> 10.7 us  [body(): lax.ppermute(packed[part], 'rep', orders[part % 2][0])]
    ppermute x6, starting transfers between devices: 7.08 us -> 5.59 us  [body(): lax.ppermute(first_sum(own[part], firsts[part]), 'rep', orders[part % 2][1])]
  transfers between devices with their start and end apart: 13 -> 13, of which waited for: 7 -> 8; matrix products, arithmetic and copies ran while one was open for 0% -> 0% of each run, Pallas kernels for 10% -> 11%
where the time goes in v4:
time: 123 us; the launch traced here: 122 us
  blocking collectives  40.3 us (33%)
  waiting for transfers between devices  34.2 us (28%)
  Pallas kernels  22.6 us (18%)
  starting transfers between devices  18.2 us (15%)
  local copies, waits for them, and re-layouts  5.98 us (5%)
    all_to_all x1, blocking collectives, body(): lax.all_to_all(pieces, ('rep', 'fsdp'), split_axis=0, concat_axis=0, tile...  40.3 us
    all_to_all x1, waiting for transfers between devices, body(): lax.all_to_all(update_block.reshape(devices, size // devices, size), ('re...  17.7 us
    ppermute x6, waiting for transfers between devices, body(): lax.ppermute(packed[part], 'rep', orders[part % 2][0])  10.7 us
    ppermute x6, starting transfers between devices, body(): lax.ppermute(packed[part], 'rep', orders[part % 2][0])  7.9 us
    pallas_call x1, Pallas kernels, statistics(): pl.pallas_call(statistics_kernel, grid=(strips,), out_shape=[jax.ShapeDty...  6.69 us
    pallas_call x1, Pallas kernels, block_update(): pl.pallas_call(functools.partial(update_kernel, tiles=tiles, out_tiles=ou...  6.32 us
    unnamed x14, local copies, waits for them, and re-layouts  5.98 us
    ppermute x6, waiting for transfers between devices, body(): lax.ppermute(first_sum(own[part], firsts[part]), 'rep', orders[part % 2][1])  5.82 us
  transfers between devices with their start and end apart: 13, of which 8 were waited for; matrix products, arithmetic and copies ran while one was open for 0% of the time, Pallas kernels for 11%

profile of v4, /device:TPU:1, one launch (start us, length us, event | category | flops | bytes accessed | tf_op | source)
XLA Modules:
  0.0 122.3 jit_solution(7607957933876326827)
XLA Ops:
  0.6 1.2 %pack.5 = (bf16[2,5,2,32,256]{4,3,2,1,0:T(8,128)(2,1)S(1)}, bf16[2,5,2,32,256]{4,3,2,1,0:T(8,128)(2,1)S(1)}) custom-call(bf16[1,12,32,5120]{3,2,1,0:T(8,128)(2,1)} %grads.7), custom_call_target="tpu_custom_call" | custom-call | tf_op jit(solution)/shard_map/pack/pallas_call | solution.py:52
  1.9 3.6 %collective-permute-start.10 = (bf16[2,5,2,32,256]{4,3,2,1,0:T(8,128)(2,1)S(1)}, bf16[2,5,2,32,256]{4,3,2,1,0:T(8,128)(2,1)S(1)}, u32[]{:S(2)}, u32[]{:S(2)}) collective-permute-start(bf16[2,5,2,32,256]{4,3,2,1,0:T(8,128)(2,1)S(1)} %get-tuple-element.44), channel_id=1, source_target_pairs={{0,96},{32,64},{64,32},{96,0},{1,97},{33,65},{65,33},{97,1},{2,98}... | collective-permute-start | bytes 983048 | tf_op jit(solution)/shard_map/ppermute | solution.py:263
  5.5 0.0 collective-permute-start.8
  5.5 1.2 %pack.4 = (bf16[2,5,2,32,256]{4,3,2,1,0:T(8,128)(2,1)S(1)}, bf16[2,5,2,32,256]{4,3,2,1,0:T(8,128)(2,1)S(1)}) custom-call(bf16[1,12,32,5120]{3,2,1,0:T(8,128)(2,1)} %grads.7), custom_call_target="tpu_custom_call" | custom-call | tf_op jit(solution)/shard_map/pack/pallas_call | solution.py:52
  6.8 1.5 %collective-permute-start.4 = (bf16[2,5,2,32,256]{4,3,2,1,0:T(8,128)(2,1)S(1)}, bf16[2,5,2,32,256]{4,3,2,1,0:T(8,128)(2,1)S(1)}, u32[]{:S(2)}, u32[]{:S(2)}) collective-permute-start(bf16[2,5,2,32,256]{4,3,2,1,0:T(8,128)(2,1)S(1)} %get-tuple-element.38), channel_id=1, source_target_pairs={{0,32},{32,0},{64,96},{96,64},{1,33},{33,1},{65,97},{97,65},{2,34}... | collective-permute-start | bytes 983048 | tf_op jit(solution)/shard_map/ppermute | solution.py:263
  8.3 0.1 collective-permute-start.6
  8.4 1.2 pack.3
  9.6 2.0 %pack_own.1 = (bf16[2,5,2,32,256]{4,3,2,1,0:T(8,128)(2,1)S(1)}, bf16[2,5,2,32,256]{4,3,2,1,0:T(8,128)(2,1)S(1)}, bf16[2,5,2,32,256]{4,3,2,1,0:T(8,128)(2,1)S(1)}...) custom-call(bf16[1,12,32,5120]{3,2,1,0:T(8,128)(2,1)} %grads.7), custom_call_target="tpu_custom_call" | custom-call | tf_op jit(solution)/shard_map/pack_own/pallas_call | solution.py:52
  11.6 0.1 collective-permute-start
  11.8 1.0 collective-permute-done.10.received.refs_4_
  12.8 2.5 %collective-permute-start.2 = (bf16[2,5,2,32,256]{4,3,2,1,0:T(8,128)(2,1)S(1)}, bf16[2,5,2,32,256]{4,3,2,1,0:T(8,128)(2,1)S(1)}, u32[]{:S(2)}, u32[]{:S(2)}) collective-permute-start(bf16[2,5,2,32,256]{4,3,2,1,0:T(8,128)(2,1)S(1)} %get-tuple-element.36), channel_id=1, source_target_pairs={{0,96},{32,64},{64,32},{96,0},{1,97},{33,65},{65,33},{97,1},{2,98}... | collective-permute-start | bytes 983048 | tf_op jit(solution)/shard_map/ppermute | solution.py:263
  15.4 0.0 copy-start.6
  15.4 0.0 collective-permute-done.8.received.refs_1_
  15.4 0.1 collective-permute-start.11
  15.5 4.3 %collective-permute-done.6.received.refs_4_ = bf16[2,5,2,32,256]{4,3,2,1,0:T(8,128)(2,1)S(1)} collective-permute-done((bf16[2,5,2,32,256]{4,3,2,1,0:T(8,128)(2,1)S(1)}, bf16[2,5,2,32,256]{4,3,2,1,0:T(8,128)(2,1)S(1)}, u32[]{:S(2)}, u32[]{:S(2)}) %collective-permute-start.6) | collective-permute-done | bytes 327712 | tf_op jit(solution)/shard_map/ppermute | solution.py:263
  19.8 2.5 %collective-permute-start.9 = (bf16[5,2,32,256]{3,2,1,0:T(8,128)(2,1)S(1)}, bf16[5,2,32,256]{3,2,1,0:T(8,128)(2,1)S(1)}, u32[]{:S(2)}, u32[]{:S(2)}) collective-permute-start(bf16[5,2,32,256]{3,2,1,0:T(8,128)(2,1)S(1)} %first_sum.10), channel_id=1, source_target_pairs={{0,96},{32,64},{64,32},{96,0},{1,97},{33,65},{65,33},{97,1},{2,98}... | collective-permute-start | bytes 491528 | tf_op jit(solution)/shard_map/ppermute | solution.py:265
  22.4 0.0 collective-permute-done.4.received.refs_1_
  22.4 0.1 collective-permute-start.7
  22.5 5.3 %collective-permute-done.received.refs_1_ = bf16[2,5,2,32,256]{4,3,2,1,0:T(8,128)(2,1)S(1)} collective-permute-done((bf16[2,5,2,32,256]{4,3,2,1,0:T(8,128)(2,1)S(1)}, bf16[2,5,2,32,256]{4,3,2,1,0:T(8,128)(2,1)S(1)}, u32[]{:S(2)}, u32[]{:S(2)}) %collective-permute-start) | collective-permute-done | bytes 327712 | tf_op jit(solution)/shard_map/ppermute | solution.py:263
  27.8 0.4 collective-permute-start.5
  28.2 0.0 collective-permute-done.2.received.refs_4_
  28.2 2.4 %collective-permute-start.1 = (bf16[5,2,32,256]{3,2,1,0:T(8,128)(2,1)S(1)}, bf16[5,2,32,256]{3,2,1,0:T(8,128)(2,1)S(1)}, u32[]{:S(2)}, u32[]{:S(2)}) collective-permute-start(bf16[5,2,32,256]{3,2,1,0:T(8,128)(2,1)S(1)} %first_sum.6), channel_id=1, source_target_pairs={{0,96},{32,64},{64,32},{96,0},{1,97},{33,65},{65,33},{97,1},{2,98}... | collective-permute-start | bytes 491528 | tf_op jit(solution)/shard_map/ppermute | solution.py:265
  30.7 0.7 collective-permute-done.11.refs_5_
  31.3 0.2 collective-permute-start.3
  31.5 0.0 copy-done.6
  31.5 0.1 select_reduce_fusion.owners
  31.6 0.0 collective-permute-done.9.refs_2_
  31.6 0.8 second_sum.3.refs_6_
  32.4 2.4 %collective-permute-done.7.refs_5_ = bf16[5,2,32,256]{3,2,1,0:T(8,128)(2,1)S(1)} collective-permute-done((bf16[5,2,32,256]{3,2,1,0:T(8,128)(2,1)S(1)}, bf16[5,2,32,256]{3,2,1,0:T(8,128)(2,1)S(1)}, u32[]{:S(2)}, u32[]{:S(2)}) %collective-permute-start.7) | collective-permute-done | bytes 163872 | tf_op jit(solution)/shard_map/ppermute | solution.py:265
  34.9 0.0 collective-permute-done.5.refs_2_
  34.9 0.7 second_sum.4.refs_6_
  35.5 0.7 collective-permute-done.1.refs_2_
  36.2 2.0 %collective-permute-done.3.refs_5_ = bf16[5,2,32,256]{3,2,1,0:T(8,128)(2,1)S(1)} collective-permute-done((bf16[5,2,32,256]{3,2,1,0:T(8,128)(2,1)S(1)}, bf16[5,2,32,256]{3,2,1,0:T(8,128)(2,1)S(1)}, u32[]{:S(2)}, u32[]{:S(2)}) %collective-permute-start.3) | collective-permute-done | bytes 163872 | tf_op jit(solution)/shard_map/ppermute | solution.py:265
  38.2 0.7 second_sum.5
  38.9 0.0 copy-start.4
  38.9 0.0 copy-start.5
  38.9 40.3 %all_to_all.10 = bf16[128,32,256]{2,1,0:T(8,128)(2,1)S(1)} all-to-all(bf16[128,32,256]{2,1,0:T(8,128)(2,1)S(1)} %second_sum.5), channel_id=1, replica_groups=mesh['rep'=4,'fsdp'=32] {'rep','fsdp'}, dimensions={0} | all-to-all | bytes 4194304 | tf_op jit(solution)/shard_map/all_to_all | solution.py:271
  79.3 0.0 copy-start
  79.3 0.0 copy-done.4
  79.3 0.0 copy-done.5
  79.3 6.3 %block_update.1 = bf16[1024,1024]{1,0:T(8,128)(2,1)} custom-call(bf16[1,1024,1024]{2,1,0:T(8,128)(2,1)S(1)} %copy-done.4, bf16[4,1024,256]{2,1,0:T(8,128)(2,1)S(1)} %bitcast.2, bf16[1,1024,1024]{2,1,0:T(8,128)(2,1)S(1)} %copy-done.5), custom_call_target="tpu_custom_call" | custom-call | flops 4294967296 | bytes 8388608 | tf_op jit(solution)/shard_map/block_update/pallas_call | solution.py:159
  85.6 0.0 copy-done
  85.6 4.7 %all-to-all-start.1 = ((bf16[128,8,1024]{2,1,0:T(8,128)(2,1)}), bf16[128,8,1024]{2,1,0:T(8,128)(2,1)S(1)}, u32[]{:S(2)}, u32[]{:S(2)}) async-start(bf16[128,8,1024]{2,1,0:T(8,128)(2,1)} %bitcast.4), calls=%async_computation.1 | async-start | bytes 4194304 | tf_op jit(solution)/shard_map/all_to_all | solution.py:274
  90.3 0.0 copy-start.1
  90.3 1.6 %copy-done.1 = bf16[128,32,256]{2,1,0:T(8,128)(2,1)S(1)} copy-done((bf16[128,32,256]{2,1,0:T(8,128)(2,1)S(1)}, bf16[128,32,256]{2,1,0:T(8,128)(2,1)}, u32[]{:S(2)}) %copy-start.1) | copy-done | bytes 2097176
  91.9 0.0 copy-start.2
  91.9 2.2 %copy-done.2 = f32[1,1024,1024]{2,1,0:T(8,128)S(1)} copy-done((f32[1,1024,1024]{2,1,0:T(8,128)S(1)}, f32[1,1024,1024]{2,1,0:T(8,128)}, u32[]{:S(2)}) %copy-start.2) | copy-done | bytes 4194328
  94.1 0.0 copy-start.3
  94.1 2.2 %copy-done.3 = f32[1,1024,1024]{2,1,0:T(8,128)S(1)} copy-done((f32[1,1024,1024]{2,1,0:T(8,128)S(1)}, f32[1,1024,1024]{2,1,0:T(8,128)}, u32[]{:S(2)}) %copy-start.3) | copy-done | bytes 4194328
  96.3 6.7 %statistics.1 = (f32[1,1024,1024]{2,1,0:T(8,128)}, f32[1,1024,1024]{2,1,0:T(8,128)}) custom-call(bf16[4,1024,256]{2,1,0:T(8,128)(2,1)S(1)} %bitcast.3, f32[1,1024,1024]{2,1,0:T(8,128)S(1)} %copy-done.2, f32[1,1024,1024]{2,1,0:T(8,128)S(1)} %copy-done.3), custom_call_target="tpu_custom_call" | custom-call | flops 4294967296 | bytes 18874368 | tf_op jit(solution)/shard_map/statistics/pallas_call | solution.py:196
  103.0 17.7 %all-to-all-done.1.returned = bf16[128,8,1024]{2,1,0:T(8,128)(2,1)S(1)} async-done(((bf16[128,8,1024]{2,1,0:T(8,128)(2,1)}), bf16[128,8,1024]{2,1,0:T(8,128)(2,1)S(1)}, u32[]{:S(2)}, u32[]{:S(2)}) %all-to-all-start.1) | async-done | bytes 2097184 | tf_op jit(solution)/shard_map/all_to_all | solution.py:274
  120.7 1.5 %pick.1 = bf16[12,8,5120]{2,1,0:T(8,128)(2,1)} custom-call(s32[60]{0:T(128)S(1)} %select_reduce_fusion.owners, bf16[128,8,1024]{2,1,0:T(8,128)(2,1)S(1)} %all-to-all-done.1.returned), custom_call_target="tpu_custom_call" | custom-call | tf_op jit(solution)/shard_map/pick/pallas_call | solution.py:226
  (6 shorter events, 0.2 us)
Async XLA Ops:
  1.9 10.9 %collective-permute-start.10 = (bf16[2,5,2,32,256]{4,3,2,1,0:T(8,128)(2,1)S(1)}, bf16[2,5,2,32,256]{4,3,2,1,0:T(8,128)(2,1)S(1)}, u32[]{:S(2)}, u32[]{:S(2)}) collective-permute-start(bf16[2,5,2,32,256]{4,3,2,1,0:T(8,128)(2,1)S(1)} %get-tuple-element.44), channel_id=1, source_target_pairs={{0,96},{32,64},{64,32},{96,0},{1,97},{33,65},{65,33},{97,1},{2,98}... | collective-permute-start | bytes 983048 | tf_op jit(solution)/shard_map/ppermute | solution.py:263
  5.5 9.8 %collective-permute-start.8 = (bf16[2,5,2,32,256]{4,3,2,1,0:T(8,128)(2,1)S(1)}, bf16[2,5,2,32,256]{4,3,2,1,0:T(8,128)(2,1)S(1)}, u32[]{:S(2)}, u32[]{:S(2)}) collective-permute-start(bf16[2,5,2,32,256]{4,3,2,1,0:T(8,128)(2,1)S(1)} %get-tuple-element.42), channel_id=1, source_target_pairs={{0,32},{32,0},{64,96},{96,64},{1,33},{33,1},{65,97},{97,65},{2,34}... | collective-permute-start | bytes 983048 | tf_op jit(solution)/shard_map/ppermute | solution.py:263
  6.8 15.6 %collective-permute-start.4 = (bf16[2,5,2,32,256]{4,3,2,1,0:T(8,128)(2,1)S(1)}, bf16[2,5,2,32,256]{4,3,2,1,0:T(8,128)(2,1)S(1)}, u32[]{:S(2)}, u32[]{:S(2)}) collective-permute-start(bf16[2,5,2,32,256]{4,3,2,1,0:T(8,128)(2,1)S(1)} %get-tuple-element.38), channel_id=1, source_target_pairs={{0,32},{32,0},{64,96},{96,64},{1,33},{33,1},{65,97},{97,65},{2,34}... | collective-permute-start | bytes 983048 | tf_op jit(solution)/shard_map/ppermute | solution.py:263
  8.3 11.5 %collective-permute-start.6 = (bf16[2,5,2,32,256]{4,3,2,1,0:T(8,128)(2,1)S(1)}, bf16[2,5,2,32,256]{4,3,2,1,0:T(8,128)(2,1)S(1)}, u32[]{:S(2)}, u32[]{:S(2)}) collective-permute-start(bf16[2,5,2,32,256]{4,3,2,1,0:T(8,128)(2,1)S(1)} %get-tuple-element.40), channel_id=1, source_target_pairs={{0,96},{32,64},{64,32},{96,0},{1,97},{33,65},{65,33},{97,1},{2,98}... | collective-permute-start | bytes 983048 | tf_op jit(solution)/shard_map/ppermute | solution.py:263
  11.6 16.2 %collective-permute-start = (bf16[2,5,2,32,256]{4,3,2,1,0:T(8,128)(2,1)S(1)}, bf16[2,5,2,32,256]{4,3,2,1,0:T(8,128)(2,1)S(1)}, u32[]{:S(2)}, u32[]{:S(2)}) collective-permute-start(bf16[2,5,2,32,256]{4,3,2,1,0:T(8,128)(2,1)S(1)} %get-tuple-element.34), channel_id=1, source_target_pairs={{0,32},{32,0},{64,96},{96,64},{1,33},{33,1},{65,97},{97,65},{2,34}... | collective-permute-start | bytes 983048 | tf_op jit(solution)/shard_map/ppermute | solution.py:263
  12.8 15.4 %collective-permute-start.2 = (bf16[2,5,2,32,256]{4,3,2,1,0:T(8,128)(2,1)S(1)}, bf16[2,5,2,32,256]{4,3,2,1,0:T(8,128)(2,1)S(1)}, u32[]{:S(2)}, u32[]{:S(2)}) collective-permute-start(bf16[2,5,2,32,256]{4,3,2,1,0:T(8,128)(2,1)S(1)} %get-tuple-element.36), channel_id=1, source_target_pairs={{0,96},{32,64},{64,32},{96,0},{1,97},{33,65},{65,33},{97,1},{2,98}... | collective-permute-start | bytes 983048 | tf_op jit(solution)/shard_map/ppermute | solution.py:263
  15.4 16.1 %copy-start.6 = (s32[128]{0:T(128)S(1)}, s32[128]{0:T(128)}, u32[]{:S(2)}) copy-start(s32[128]{0:T(128)} %param.11) | copy-start | bytes 1540
  15.4 16.0 %collective-permute-start.11 = (bf16[5,2,32,256]{3,2,1,0:T(8,128)(2,1)S(1)}, bf16[5,2,32,256]{3,2,1,0:T(8,128)(2,1)S(1)}, u32[]{:S(2)}, u32[]{:S(2)}) collective-permute-start(bf16[5,2,32,256]{3,2,1,0:T(8,128)(2,1)S(1)} %first_sum.11), channel_id=1, source_target_pairs={{0,32},{32,0},{64,96},{96,64},{1,33},{33,1},{65,97},{97,65},{2,34}... | collective-permute-start | bytes 491528 | tf_op jit(solution)/shard_map/ppermute | solution.py:265
  19.8 11.8 %collective-permute-start.9 = (bf16[5,2,32,256]{3,2,1,0:T(8,128)(2,1)S(1)}, bf16[5,2,32,256]{3,2,1,0:T(8,128)(2,1)S(1)}, u32[]{:S(2)}, u32[]{:S(2)}) collective-permute-start(bf16[5,2,32,256]{3,2,1,0:T(8,128)(2,1)S(1)} %first_sum.10), channel_id=1, source_target_pairs={{0,96},{32,64},{64,32},{96,0},{1,97},{33,65},{65,33},{97,1},{2,98}... | collective-permute-start | bytes 491528 | tf_op jit(solution)/shard_map/ppermute | solution.py:265
  22.4 12.5 %collective-permute-start.7 = (bf16[5,2,32,256]{3,2,1,0:T(8,128)(2,1)S(1)}, bf16[5,2,32,256]{3,2,1,0:T(8,128)(2,1)S(1)}, u32[]{:S(2)}, u32[]{:S(2)}) collective-permute-start(bf16[5,2,32,256]{3,2,1,0:T(8,128)(2,1)S(1)} %first_sum.9), channel_id=1, source_target_pairs={{0,32},{32,0},{64,96},{96,64},{1,33},{33,1},{65,97},{97,65},{2,34}... | collective-permute-start | bytes 491528 | tf_op jit(solution)/shard_map/ppermute | solution.py:265
  27.8 7.0 %collective-permute-start.5 = (bf16[5,2,32,256]{3,2,1,0:T(8,128)(2,1)S(1)}, bf16[5,2,32,256]{3,2,1,0:T(8,128)(2,1)S(1)}, u32[]{:S(2)}, u32[]{:S(2)}) collective-permute-start(bf16[5,2,32,256]{3,2,1,0:T(8,128)(2,1)S(1)} %first_sum.8), channel_id=1, source_target_pairs={{0,96},{32,64},{64,32},{96,0},{1,97},{33,65},{65,33},{97,1},{2,98}... | collective-permute-start | bytes 491528 | tf_op jit(solution)/shard_map/ppermute | solution.py:265
  28.2 8.0 %collective-permute-start.1 = (bf16[5,2,32,256]{3,2,1,0:T(8,128)(2,1)S(1)}, bf16[5,2,32,256]{3,2,1,0:T(8,128)(2,1)S(1)}, u32[]{:S(2)}, u32[]{:S(2)}) collective-permute-start(bf16[5,2,32,256]{3,2,1,0:T(8,128)(2,1)S(1)} %first_sum.6), channel_id=1, source_target_pairs={{0,96},{32,64},{64,32},{96,0},{1,97},{33,65},{65,33},{97,1},{2,98}... | collective-permute-start | bytes 491528 | tf_op jit(solution)/shard_map/ppermute | solution.py:265
  31.3 6.9 %collective-permute-start.3 = (bf16[5,2,32,256]{3,2,1,0:T(8,128)(2,1)S(1)}, bf16[5,2,32,256]{3,2,1,0:T(8,128)(2,1)S(1)}, u32[]{:S(2)}, u32[]{:S(2)}) collective-permute-start(bf16[5,2,32,256]{3,2,1,0:T(8,128)(2,1)S(1)} %first_sum.7), channel_id=1, source_target_pairs={{0,32},{32,0},{64,96},{96,64},{1,33},{33,1},{65,97},{97,65},{2,34}... | collective-permute-start | bytes 491528 | tf_op jit(solution)/shard_map/ppermute | solution.py:265
  38.9 40.3 %copy-start.4 = (bf16[1,1024,1024]{2,1,0:T(8,128)(2,1)S(1)}, bf16[1,1024,1024]{2,1,0:T(8,128)(2,1)}, u32[]{:S(2)}) copy-start(bf16[1,1024,1024]{2,1,0:T(8,128)(2,1)} %left.3) | copy-start | bytes 6291460
  38.9 40.3 %copy-start.5 = (bf16[1,1024,1024]{2,1,0:T(8,128)(2,1)S(1)}, bf16[1,1024,1024]{2,1,0:T(8,128)(2,1)}, u32[]{:S(2)}) copy-start(bf16[1,1024,1024]{2,1,0:T(8,128)(2,1)} %right.3) | copy-start | bytes 6291460
  79.3 6.3 %copy-start = (bf16[128,32,256]{2,1,0:T(8,128)(2,1)}, bf16[128,32,256]{2,1,0:T(8,128)(2,1)S(1)}, u32[]{:S(2)}) copy-start(bf16[128,32,256]{2,1,0:T(8,128)(2,1)S(1)} %all_to_all.10) | copy-start | bytes 6291460
  85.6 35.1 %all-to-all-start.1 = ((bf16[128,8,1024]{2,1,0:T(8,128)(2,1)}), bf16[128,8,1024]{2,1,0:T(8,128)(2,1)S(1)}, u32[]{:S(2)}, u32[]{:S(2)}) async-start(bf16[128,8,1024]{2,1,0:T(8,128)(2,1)} %bitcast.4), calls=%async_computation.1 | async-start | bytes 4194304 | tf_op jit(solution)/shard_map/all_to_all | solution.py:274
  90.3 1.6 %copy-start.1 = (bf16[128,32,256]{2,1,0:T(8,128)(2,1)S(1)}, bf16[128,32,256]{2,1,0:T(8,128)(2,1)}, u32[]{:S(2)}) copy-start(bf16[128,32,256]{2,1,0:T(8,128)(2,1)} %copy-done) | copy-start | bytes 6291460
  91.9 2.2 %copy-start.2 = (f32[1,1024,1024]{2,1,0:T(8,128)S(1)}, f32[1,1024,1024]{2,1,0:T(8,128)}, u32[]{:S(2)}) copy-start(f32[1,1024,1024]{2,1,0:T(8,128)} %left.2) | copy-start | bytes 12582916
  94.1 2.2 %copy-start.3 = (f32[1,1024,1024]{2,1,0:T(8,128)S(1)}, f32[1,1024,1024]{2,1,0:T(8,128)}, u32[]{:S(2)}) copy-start(f32[1,1024,1024]{2,1,0:T(8,128)} %right.2) | copy-start | bytes 12582916

commit v5 on v4

--- a/solution.py
+++ b/solution.py
@@ -258,9 +258,8 @@
     pairs = [(2 * stage, 2 * stage + 1) for stage in range(stages)]
     sizes = (columns, reps, width)
     packed = [part for pair in pairs for part in pack(grads, pair, spans, False, *sizes)]
+    firsts = [lax.ppermute(packed[part], "rep", orders[part % 2][0]) for part in parts]
     own = pack(grads, tuple(parts), spans, True, *sizes)
-    packed[-2:], own = lax.optimization_barrier((packed[-2:], own))
-    firsts = [lax.ppermute(packed[part], "rep", orders[part % 2][0]) for part in parts]
     seconds = [
         lax.ppermute(first_sum(own[part], firsts[part]), "rep", orders[part % 2][1]) for part in parts
     ]

time: 123 us -> 123 us (level)
    ppermute x6, waiting for transfers between devices: 10.7 us -> 8.81 us  [body(): lax.ppermute(packed[part], 'rep', orders[part % 2][0])]
    ppermute x6, starting transfers between devices: 5.59 us -> 7.08 us  [body(): lax.ppermute(first_sum(own[part], firsts[part]), 'rep', orders[part % 2][1])]
  transfers between devices with their start and end apart: 13 -> 13, of which waited for: 8 -> 7; matrix products, arithmetic and copies ran while one was open for 0% -> 0% of each run, Pallas kernels for 11% -> 10%
where the time goes in v5:
time: 123 us; the launch traced here: 122 us
  blocking collectives  40.2 us (33%)
  waiting for transfers between devices  33.4 us (27%)
  Pallas kernels  22.6 us (18%)
  starting transfers between devices  19.1 us (16%)
  local copies, waits for them, and re-layouts  5.98 us (5%)
    all_to_all x1, blocking collectives, body(): lax.all_to_all(pieces, ('rep', 'fsdp'), split_axis=0, concat_axis=0, tile...  40.2 us
    all_to_all x1, waiting for transfers between devices, body(): lax.all_to_all(update_block.reshape(devices, size // devices, size), ('re...  17.7 us
    ppermute x6, waiting for transfers between devices, body(): lax.ppermute(packed[part], 'rep', orders[part % 2][0])  8.81 us
    ppermute x6, starting transfers between devices, body(): lax.ppermute(packed[part], 'rep', orders[part % 2][0])  7.34 us
    ppermute x6, starting transfers between devices, body(): lax.ppermute(first_sum(own[part], firsts[part]), 'rep', orders[part % 2][1])  7.08 us
    ppermute x6, waiting for transfers between devices, body(): lax.ppermute(first_sum(own[part], firsts[part]), 'rep', orders[part % 2][1])  6.88 us
    pallas_call x1, Pallas kernels, statistics(): pl.pallas_call(statistics_kernel, grid=(strips,), out_shape=[jax.ShapeDty...  6.69 us
    pallas_call x1, Pallas kernels, block_update(): pl.pallas_call(functools.partial(update_kernel, tiles=tiles, out_tiles=ou...  6.32 us
  transfers between devices with their start and end apart: 13, of which 7 were waited for; matrix products, arithmetic and copies ran while one was open for 0% of the time, Pallas kernels for 10%

profile of v5, /device:TPU:1, one launch (start us, length us, event | category | flops | bytes accessed | tf_op | source)
XLA Modules:
  0.0 122.3 jit_solution(3520972214930810307)
XLA Ops:
  0.6 1.2 %pack.5 = (bf16[2,5,2,32,256]{4,3,2,1,0:T(8,128)(2,1)S(1)}, bf16[2,5,2,32,256]{4,3,2,1,0:T(8,128)(2,1)S(1)}) custom-call(bf16[1,12,32,5120]{3,2,1,0:T(8,128)(2,1)} %grads.7), custom_call_target="tpu_custom_call" | custom-call | tf_op jit(solution)/shard_map/pack/pallas_call | solution.py:52
  1.9 3.6 %collective-permute-start.10 = (bf16[2,5,2,32,256]{4,3,2,1,0:T(8,128)(2,1)S(1)}, bf16[2,5,2,32,256]{4,3,2,1,0:T(8,128)(2,1)S(1)}, u32[]{:S(2)}, u32[]{:S(2)}) collective-permute-start(bf16[2,5,2,32,256]{4,3,2,1,0:T(8,128)(2,1)S(1)} %get-tuple-element.28), channel_id=1, source_target_pairs={{0,96},{32,64},{64,32},{96,0},{1,97},{33,65},{65,33},{97,1},{2,98}... | collective-permute-start | bytes 983048 | tf_op jit(solution)/shard_map/ppermute | solution.py:261
  5.5 0.0 collective-permute-start.8
  5.5 1.2 %pack.4 = (bf16[2,5,2,32,256]{4,3,2,1,0:T(8,128)(2,1)S(1)}, bf16[2,5,2,32,256]{4,3,2,1,0:T(8,128)(2,1)S(1)}) custom-call(bf16[1,12,32,5120]{3,2,1,0:T(8,128)(2,1)} %grads.7), custom_call_target="tpu_custom_call" | custom-call | tf_op jit(solution)/shard_map/pack/pallas_call | solution.py:52
  6.8 0.7 collective-permute-start.6
  7.5 0.9 collective-permute-start.4
  8.4 1.2 pack.3
  9.6 2.1 %collective-permute-start.2 = (bf16[2,5,2,32,256]{4,3,2,1,0:T(8,128)(2,1)S(1)}, bf16[2,5,2,32,256]{4,3,2,1,0:T(8,128)(2,1)S(1)}, u32[]{:S(2)}, u32[]{:S(2)}) collective-permute-start(bf16[2,5,2,32,256]{4,3,2,1,0:T(8,128)(2,1)S(1)} %get-tuple-element.20), channel_id=1, source_target_pairs={{0,96},{32,64},{64,32},{96,0},{1,97},{33,65},{65,33},{97,1},{2,98}... | collective-permute-start | bytes 983048 | tf_op jit(solution)/shard_map/ppermute | solution.py:261
  11.7 1.1 collective-permute-done.10.received.refs_4_
  12.8 0.0 collective-permute-start
  12.8 2.0 %pack_own.1 = (bf16[2,5,2,32,256]{4,3,2,1,0:T(8,128)(2,1)S(1)}, bf16[2,5,2,32,256]{4,3,2,1,0:T(8,128)(2,1)S(1)}, bf16[2,5,2,32,256]{4,3,2,1,0:T(8,128)(2,1)S(1)}...) custom-call(bf16[1,12,32,5120]{3,2,1,0:T(8,128)(2,1)} %grads.7), custom_call_target="tpu_custom_call" | custom-call | tf_op jit(solution)/shard_map/pack_own/pallas_call | solution.py:52
  14.9 0.0 copy-start.6
  14.9 0.0 collective-permute-done.8.received.refs_1_
  14.9 1.5 %collective-permute-start.11 = (bf16[5,2,32,256]{3,2,1,0:T(8,128)(2,1)S(1)}, bf16[5,2,32,256]{3,2,1,0:T(8,128)(2,1)S(1)}, u32[]{:S(2)}, u32[]{:S(2)}) collective-permute-start(bf16[5,2,32,256]{3,2,1,0:T(8,128)(2,1)S(1)} %first_sum.11), channel_id=1, source_target_pairs={{0,32},{32,0},{64,96},{96,64},{1,33},{33,1},{65,97},{97,65},{2,34}... | collective-permute-start | bytes 491528 | tf_op jit(solution)/shard_map/ppermute | solution.py:264
  16.5 3.4 %collective-permute-done.6.received.refs_4_ = bf16[2,5,2,32,256]{4,3,2,1,0:T(8,128)(2,1)S(1)} collective-permute-done((bf16[2,5,2,32,256]{4,3,2,1,0:T(8,128)(2,1)S(1)}, bf16[2,5,2,32,256]{4,3,2,1,0:T(8,128)(2,1)S(1)}, u32[]{:S(2)}, u32[]{:S(2)}) %collective-permute-start.6) | collective-permute-done | bytes 327712 | tf_op jit(solution)/shard_map/ppermute | solution.py:261
  19.8 2.5 %collective-permute-start.9 = (bf16[5,2,32,256]{3,2,1,0:T(8,128)(2,1)S(1)}, bf16[5,2,32,256]{3,2,1,0:T(8,128)(2,1)S(1)}, u32[]{:S(2)}, u32[]{:S(2)}) collective-permute-start(bf16[5,2,32,256]{3,2,1,0:T(8,128)(2,1)S(1)} %first_sum.10), channel_id=1, source_target_pairs={{0,96},{32,64},{64,32},{96,0},{1,97},{33,65},{65,33},{97,1},{2,98}... | collective-permute-start | bytes 491528 | tf_op jit(solution)/shard_map/ppermute | solution.py:264
  22.4 0.0 collective-permute-done.4.received.refs_1_
  22.4 0.1 collective-permute-start.7
  22.5 4.3 %collective-permute-done.2.received.refs_4_ = bf16[2,5,2,32,256]{4,3,2,1,0:T(8,128)(2,1)S(1)} collective-permute-done((bf16[2,5,2,32,256]{4,3,2,1,0:T(8,128)(2,1)S(1)}, bf16[2,5,2,32,256]{4,3,2,1,0:T(8,128)(2,1)S(1)}, u32[]{:S(2)}, u32[]{:S(2)}) %collective-permute-start.2) | collective-permute-done | bytes 327712 | tf_op jit(solution)/shard_map/ppermute | solution.py:261
  26.9 2.5 %collective-permute-start.5 = (bf16[5,2,32,256]{3,2,1,0:T(8,128)(2,1)S(1)}, bf16[5,2,32,256]{3,2,1,0:T(8,128)(2,1)S(1)}, u32[]{:S(2)}, u32[]{:S(2)}) collective-permute-start(bf16[5,2,32,256]{3,2,1,0:T(8,128)(2,1)S(1)} %first_sum.8), channel_id=1, source_target_pairs={{0,96},{32,64},{64,32},{96,0},{1,97},{33,65},{65,33},{97,1},{2,98}... | collective-permute-start | bytes 491528 | tf_op jit(solution)/shard_map/ppermute | solution.py:264
  29.4 0.0 collective-permute-done.received.refs_1_
  29.4 0.1 collective-permute-start.3
  29.6 1.8 %collective-permute-done.11.refs_5_ = bf16[5,2,32,256]{3,2,1,0:T(8,128)(2,1)S(1)} collective-permute-done((bf16[5,2,32,256]{3,2,1,0:T(8,128)(2,1)S(1)}, bf16[5,2,32,256]{3,2,1,0:T(8,128)(2,1)S(1)}, u32[]{:S(2)}, u32[]{:S(2)}) %collective-permute-start.11) | collective-permute-done | bytes 163872 | tf_op jit(solution)/shard_map/ppermute | solution.py:264
  31.3 0.4 collective-permute-start.1
  31.7 0.0 copy-done.6
  31.7 0.1 select_reduce_fusion.owners
  31.8 0.0 collective-permute-done.9.refs_2_
  31.8 0.8 second_sum.3.refs_6_
  32.6 2.2 %collective-permute-done.7.refs_5_ = bf16[5,2,32,256]{3,2,1,0:T(8,128)(2,1)S(1)} collective-permute-done((bf16[5,2,32,256]{3,2,1,0:T(8,128)(2,1)S(1)}, bf16[5,2,32,256]{3,2,1,0:T(8,128)(2,1)S(1)}, u32[]{:S(2)}, u32[]{:S(2)}) %collective-permute-start.7) | collective-permute-done | bytes 163872 | tf_op jit(solution)/shard_map/ppermute | solution.py:264
  34.9 0.0 collective-permute-done.5.refs_2_
  34.9 0.7 second_sum.4.refs_6_
  35.5 2.8 %collective-permute-done.3.refs_5_ = bf16[5,2,32,256]{3,2,1,0:T(8,128)(2,1)S(1)} collective-permute-done((bf16[5,2,32,256]{3,2,1,0:T(8,128)(2,1)S(1)}, bf16[5,2,32,256]{3,2,1,0:T(8,128)(2,1)S(1)}, u32[]{:S(2)}, u32[]{:S(2)}) %collective-permute-start.3) | collective-permute-done | bytes 163872 | tf_op jit(solution)/shard_map/ppermute | solution.py:264
  38.4 0.0 collective-permute-done.1.refs_2_
  38.4 0.7 second_sum.5
  39.0 0.0 copy-start.4
  39.0 0.0 copy-start.5
  39.1 40.2 %all_to_all.10 = bf16[128,32,256]{2,1,0:T(8,128)(2,1)S(1)} all-to-all(bf16[128,32,256]{2,1,0:T(8,128)(2,1)S(1)} %second_sum.5), channel_id=1, replica_groups=mesh['rep'=4,'fsdp'=32] {'rep','fsdp'}, dimensions={0} | all-to-all | bytes 4194304 | tf_op jit(solution)/shard_map/all_to_all | solution.py:270
  79.3 0.0 copy-start
  79.3 0.0 copy-done.4
  79.3 0.0 copy-done.5
  79.3 6.3 %block_update.1 = bf16[1024,1024]{1,0:T(8,128)(2,1)} custom-call(bf16[1,1024,1024]{2,1,0:T(8,128)(2,1)S(1)} %copy-done.4, bf16[4,1024,256]{2,1,0:T(8,128)(2,1)S(1)} %bitcast.2, bf16[1,1024,1024]{2,1,0:T(8,128)(2,1)S(1)} %copy-done.5), custom_call_target="tpu_custom_call" | custom-call | flops 4294967296 | bytes 8388608 | tf_op jit(solution)/shard_map/block_update/pallas_call | solution.py:159
  85.6 0.0 copy-done
  85.6 4.7 %all-to-all-start.1 = ((bf16[128,8,1024]{2,1,0:T(8,128)(2,1)}), bf16[128,8,1024]{2,1,0:T(8,128)(2,1)S(1)}, u32[]{:S(2)}, u32[]{:S(2)}) async-start(bf16[128,8,1024]{2,1,0:T(8,128)(2,1)} %bitcast.4), calls=%async_computation.1 | async-start | bytes 4194304 | tf_op jit(solution)/shard_map/all_to_all | solution.py:273
  90.4 0.0 copy-start.1
  90.4 1.6 %copy-done.1 = bf16[128,32,256]{2,1,0:T(8,128)(2,1)S(1)} copy-done((bf16[128,32,256]{2,1,0:T(8,128)(2,1)S(1)}, bf16[128,32,256]{2,1,0:T(8,128)(2,1)}, u32[]{:S(2)}) %copy-start.1) | copy-done | bytes 2097176
  92.0 0.0 copy-start.2
  92.0 2.2 %copy-done.2 = f32[1,1024,1024]{2,1,0:T(8,128)S(1)} copy-done((f32[1,1024,1024]{2,1,0:T(8,128)S(1)}, f32[1,1024,1024]{2,1,0:T(8,128)}, u32[]{:S(2)}) %copy-start.2) | copy-done | bytes 4194328
  94.2 0.0 copy-start.3
  94.2 2.2 %copy-done.3 = f32[1,1024,1024]{2,1,0:T(8,128)S(1)} copy-done((f32[1,1024,1024]{2,1,0:T(8,128)S(1)}, f32[1,1024,1024]{2,1,0:T(8,128)}, u32[]{:S(2)}) %copy-start.3) | copy-done | bytes 4194328
  96.3 6.7 %statistics.1 = (f32[1,1024,1024]{2,1,0:T(8,128)}, f32[1,1024,1024]{2,1,0:T(8,128)}) custom-call(bf16[4,1024,256]{2,1,0:T(8,128)(2,1)S(1)} %bitcast.3, f32[1,1024,1024]{2,1,0:T(8,128)S(1)} %copy-done.2, f32[1,1024,1024]{2,1,0:T(8,128)S(1)} %copy-done.3), custom_call_target="tpu_custom_call" | custom-call | flops 4294967296 | bytes 18874368 | tf_op jit(solution)/shard_map/statistics/pallas_call | solution.py:196
  103.0 17.7 %all-to-all-done.1.returned = bf16[128,8,1024]{2,1,0:T(8,128)(2,1)S(1)} async-done(((bf16[128,8,1024]{2,1,0:T(8,128)(2,1)}), bf16[128,8,1024]{2,1,0:T(8,128)(2,1)S(1)}, u32[]{:S(2)}, u32[]{:S(2)}) %all-to-all-start.1) | async-done | bytes 2097184 | tf_op jit(solution)/shard_map/all_to_all | solution.py:273
  120.8 1.5 %pick.1 = bf16[12,8,5120]{2,1,0:T(8,128)(2,1)} custom-call(s32[60]{0:T(128)S(1)} %select_reduce_fusion.owners, bf16[128,8,1024]{2,1,0:T(8,128)(2,1)S(1)} %all-to-all-done.1.returned), custom_call_target="tpu_custom_call" | custom-call | tf_op jit(solution)/shard_map/pick/pallas_call | solution.py:226
  (6 shorter events, 0.2 us)
Async XLA Ops:
  1.9 10.9 %collective-permute-start.10 = (bf16[2,5,2,32,256]{4,3,2,1,0:T(8,128)(2,1)S(1)}, bf16[2,5,2,32,256]{4,3,2,1,0:T(8,128)(2,1)S(1)}, u32[]{:S(2)}, u32[]{:S(2)}) collective-permute-start(bf16[2,5,2,32,256]{4,3,2,1,0:T(8,128)(2,1)S(1)} %get-tuple-element.28), channel_id=1, source_target_pairs={{0,96},{32,64},{64,32},{96,0},{1,97},{33,65},{65,33},{97,1},{2,98}... | collective-permute-start | bytes 983048 | tf_op jit(solution)/shard_map/ppermute | solution.py:261
  5.5 9.4 %collective-permute-start.8 = (bf16[2,5,2,32,256]{4,3,2,1,0:T(8,128)(2,1)S(1)}, bf16[2,5,2,32,256]{4,3,2,1,0:T(8,128)(2,1)S(1)}, u32[]{:S(2)}, u32[]{:S(2)}) collective-permute-start(bf16[2,5,2,32,256]{4,3,2,1,0:T(8,128)(2,1)S(1)} %get-tuple-element.26), channel_id=1, source_target_pairs={{0,32},{32,0},{64,96},{96,64},{1,33},{33,1},{65,97},{97,65},{2,34}... | collective-permute-start | bytes 983048 | tf_op jit(solution)/shard_map/ppermute | solution.py:261
  6.8 13.1 %collective-permute-start.6 = (bf16[2,5,2,32,256]{4,3,2,1,0:T(8,128)(2,1)S(1)}, bf16[2,5,2,32,256]{4,3,2,1,0:T(8,128)(2,1)S(1)}, u32[]{:S(2)}, u32[]{:S(2)}) collective-permute-start(bf16[2,5,2,32,256]{4,3,2,1,0:T(8,128)(2,1)S(1)} %get-tuple-element.24), channel_id=1, source_target_pairs={{0,96},{32,64},{64,32},{96,0},{1,97},{33,65},{65,33},{97,1},{2,98}... | collective-permute-start | bytes 983048 | tf_op jit(solution)/shard_map/ppermute | solution.py:261
  7.5 14.9 %collective-permute-start.4 = (bf16[2,5,2,32,256]{4,3,2,1,0:T(8,128)(2,1)S(1)}, bf16[2,5,2,32,256]{4,3,2,1,0:T(8,128)(2,1)S(1)}, u32[]{:S(2)}, u32[]{:S(2)}) collective-permute-start(bf16[2,5,2,32,256]{4,3,2,1,0:T(8,128)(2,1)S(1)} %get-tuple-element.22), channel_id=1, source_target_pairs={{0,32},{32,0},{64,96},{96,64},{1,33},{33,1},{65,97},{97,65},{2,34}... | collective-permute-start | bytes 983048 | tf_op jit(solution)/shard_map/ppermute | solution.py:261
  9.6 17.2 %collective-permute-start.2 = (bf16[2,5,2,32,256]{4,3,2,1,0:T(8,128)(2,1)S(1)}, bf16[2,5,2,32,256]{4,3,2,1,0:T(8,128)(2,1)S(1)}, u32[]{:S(2)}, u32[]{:S(2)}) collective-permute-start(bf16[2,5,2,32,256]{4,3,2,1,0:T(8,128)(2,1)S(1)} %get-tuple-element.20), channel_id=1, source_target_pairs={{0,96},{32,64},{64,32},{96,0},{1,97},{33,65},{65,33},{97,1},{2,98}... | collective-permute-start | bytes 983048 | tf_op jit(solution)/shard_map/ppermute | solution.py:261
  12.8 16.6 %collective-permute-start = (bf16[2,5,2,32,256]{4,3,2,1,0:T(8,128)(2,1)S(1)}, bf16[2,5,2,32,256]{4,3,2,1,0:T(8,128)(2,1)S(1)}, u32[]{:S(2)}, u32[]{:S(2)}) collective-permute-start(bf16[2,5,2,32,256]{4,3,2,1,0:T(8,128)(2,1)S(1)} %get-tuple-element.18), channel_id=1, source_target_pairs={{0,32},{32,0},{64,96},{96,64},{1,33},{33,1},{65,97},{97,65},{2,34}... | collective-permute-start | bytes 983048 | tf_op jit(solution)/shard_map/ppermute | solution.py:261
  14.9 16.8 %copy-start.6 = (s32[128]{0:T(128)S(1)}, s32[128]{0:T(128)}, u32[]{:S(2)}) copy-start(s32[128]{0:T(128)} %param.11) | copy-start | bytes 1540
  14.9 16.5 %collective-permute-start.11 = (bf16[5,2,32,256]{3,2,1,0:T(8,128)(2,1)S(1)}, bf16[5,2,32,256]{3,2,1,0:T(8,128)(2,1)S(1)}, u32[]{:S(2)}, u32[]{:S(2)}) collective-permute-start(bf16[5,2,32,256]{3,2,1,0:T(8,128)(2,1)S(1)} %first_sum.11), channel_id=1, source_target_pairs={{0,32},{32,0},{64,96},{96,64},{1,33},{33,1},{65,97},{97,65},{2,34}... | collective-permute-start | bytes 491528 | tf_op jit(solution)/shard_map/ppermute | solution.py:264
  19.8 12.0 %collective-permute-start.9 = (bf16[5,2,32,256]{3,2,1,0:T(8,128)(2,1)S(1)}, bf16[5,2,32,256]{3,2,1,0:T(8,128)(2,1)S(1)}, u32[]{:S(2)}, u32[]{:S(2)}) collective-permute-start(bf16[5,2,32,256]{3,2,1,0:T(8,128)(2,1)S(1)} %first_sum.10), channel_id=1, source_target_pairs={{0,96},{32,64},{64,32},{96,0},{1,97},{33,65},{65,33},{97,1},{2,98}... | collective-permute-start | bytes 491528 | tf_op jit(solution)/shard_map/ppermute | solution.py:264
  22.4 12.5 %collective-permute-start.7 = (bf16[5,2,32,256]{3,2,1,0:T(8,128)(2,1)S(1)}, bf16[5,2,32,256]{3,2,1,0:T(8,128)(2,1)S(1)}, u32[]{:S(2)}, u32[]{:S(2)}) collective-permute-start(bf16[5,2,32,256]{3,2,1,0:T(8,128)(2,1)S(1)} %first_sum.9), channel_id=1, source_target_pairs={{0,32},{32,0},{64,96},{96,64},{1,33},{33,1},{65,97},{97,65},{2,34}... | collective-permute-start | bytes 491528 | tf_op jit(solution)/shard_map/ppermute | solution.py:264
  26.9 8.0 %collective-permute-start.5 = (bf16[5,2,32,256]{3,2,1,0:T(8,128)(2,1)S(1)}, bf16[5,2,32,256]{3,2,1,0:T(8,128)(2,1)S(1)}, u32[]{:S(2)}, u32[]{:S(2)}) collective-permute-start(bf16[5,2,32,256]{3,2,1,0:T(8,128)(2,1)S(1)} %first_sum.8), channel_id=1, source_target_pairs={{0,96},{32,64},{64,32},{96,0},{1,97},{33,65},{65,33},{97,1},{2,98}... | collective-permute-start | bytes 491528 | tf_op jit(solution)/shard_map/ppermute | solution.py:264
  29.4 9.0 %collective-permute-start.3 = (bf16[5,2,32,256]{3,2,1,0:T(8,128)(2,1)S(1)}, bf16[5,2,32,256]{3,2,1,0:T(8,128)(2,1)S(1)}, u32[]{:S(2)}, u32[]{:S(2)}) collective-permute-start(bf16[5,2,32,256]{3,2,1,0:T(8,128)(2,1)S(1)} %first_sum.7), channel_id=1, source_target_pairs={{0,32},{32,0},{64,96},{96,64},{1,33},{33,1},{65,97},{97,65},{2,34}... | collective-permute-start | bytes 491528 | tf_op jit(solution)/shard_map/ppermute | solution.py:264
  31.3 7.0 %collective-permute-start.1 = (bf16[5,2,32,256]{3,2,1,0:T(8,128)(2,1)S(1)}, bf16[5,2,32,256]{3,2,1,0:T(8,128)(2,1)S(1)}, u32[]{:S(2)}, u32[]{:S(2)}) collective-permute-start(bf16[5,2,32,256]{3,2,1,0:T(8,128)(2,1)S(1)} %first_sum.6), channel_id=1, source_target_pairs={{0,96},{32,64},{64,32},{96,0},{1,97},{33,65},{65,33},{97,1},{2,98}... | collective-permute-start | bytes 491528 | tf_op jit(solution)/shard_map/ppermute | solution.py:264
  39.0 40.3 %copy-start.4 = (bf16[1,1024,1024]{2,1,0:T(8,128)(2,1)S(1)}, bf16[1,1024,1024]{2,1,0:T(8,128)(2,1)}, u32[]{:S(2)}) copy-start(bf16[1,1024,1024]{2,1,0:T(8,128)(2,1)} %left.3) | copy-start | bytes 6291460
  39.0 40.3 %copy-start.5 = (bf16[1,1024,1024]{2,1,0:T(8,128)(2,1)S(1)}, bf16[1,1024,1024]{2,1,0:T(8,128)(2,1)}, u32[]{:S(2)}) copy-start(bf16[1,1024,1024]{2,1,0:T(8,128)(2,1)} %right.3) | copy-start | bytes 6291460
  79.3 6.3 %copy-start = (bf16[128,32,256]{2,1,0:T(8,128)(2,1)}, bf16[128,32,256]{2,1,0:T(8,128)(2,1)S(1)}, u32[]{:S(2)}) copy-start(bf16[128,32,256]{2,1,0:T(8,128)(2,1)S(1)} %all_to_all.10) | copy-start | bytes 6291460
  85.6 35.1 %all-to-all-start.1 = ((bf16[128,8,1024]{2,1,0:T(8,128)(2,1)}), bf16[128,8,1024]{2,1,0:T(8,128)(2,1)S(1)}, u32[]{:S(2)}, u32[]{:S(2)}) async-start(bf16[128,8,1024]{2,1,0:T(8,128)(2,1)} %bitcast.4), calls=%async_computation.1 | async-start | bytes 4194304 | tf_op jit(solution)/shard_map/all_to_all | solution.py:273
  90.4 1.6 %copy-start.1 = (bf16[128,32,256]{2,1,0:T(8,128)(2,1)S(1)}, bf16[128,32,256]{2,1,0:T(8,128)(2,1)}, u32[]{:S(2)}) copy-start(bf16[128,32,256]{2,1,0:T(8,128)(2,1)} %copy-done) | copy-start | bytes 6291460
  92.0 2.2 %copy-start.2 = (f32[1,1024,1024]{2,1,0:T(8,128)S(1)}, f32[1,1024,1024]{2,1,0:T(8,128)}, u32[]{:S(2)}) copy-start(f32[1,1024,1024]{2,1,0:T(8,128)} %left.2) | copy-start | bytes 12582916
  94.2 2.2 %copy-start.3 = (f32[1,1024,1024]{2,1,0:T(8,128)S(1)}, f32[1,1024,1024]{2,1,0:T(8,128)}, u32[]{:S(2)}) copy-start(f32[1,1024,1024]{2,1,0:T(8,128)} %right.2) | copy-start | bytes 12582916
